TPU v7x, 32 devices: a whole 2x2x4 slice. The times are simulated.
32 devices in a mesh: dp: 8 (over z, core), space: 4 (over y, x).
Axes of the slice: x: 2, y: 2, z: 4, core: 2. Of those that a mesh axis runs over, the one named last changes fastest.
Arguments:
- query: bfloat16 [8, 1536, 1536], P('dp', 'space'), may hold values from -8 to 8
- key_in: bfloat16 [8, 1536, 1536], P('dp', 'space'), may hold values from -8 to 8
- value_in: bfloat16 [8, 1536, 1536], P('dp', 'space'), may hold values from -6 to 6
- out_weight: bfloat16 [1536, 3072], P('dp'), may hold values from -0.15625 to 0.15625
- grad_out: bfloat16 [8, 1536, 3072], P('dp', 'space'), may hold values from -6 to 6
- neighbours: int32 [4, 3], replicated, may hold values from -1 to 3, as said below
Outputs:
- mixed: bfloat16 [8, 1536, 3072], P('dp', 'space')
- grad_query: bfloat16 [8, 1536, 1536], P('dp', 'space')
- grad_key: bfloat16 [8, 1536, 1536], P('dp', 'space')
- grad_value: bfloat16 [8, 1536, 1536], P('dp', 'space')
- grad_weight: float32 [1536, 3072], P('dp')
Inputs may be any that keep to these rules, and one draw needn't show every extreme that they name: `neighbours`: entry 0 of row t is t; entry 1 is t - 1 or -1; entry 2 is t + 1 or -1.
All inputs are finite; a program needn't handle non-finite values.
Results may differ from a plain program's by a relative error of at most 0.034.
Values may be sent and summed in bfloat16 or wider, within the bound.
A program may use at most 192 MiB of HBM per device.

v0:
```python
import math

import jax
import jax.numpy as jnp
from jax import lax
from jax.sharding import PartitionSpec as P

HEAD = 128


masked_score = -1e30


def padded(x, sides, width):
    for axis, dim in sides:
        size, length = (lax.axis_size(axis), x.shape[dim])
        up = [(i, (i + 1) % size) for i in range(size - 1)]
        down = [(j, i) for i, j in up]
        last = lax.slice_in_dim(x, length - width, length, axis=dim)
        initial = lax.slice_in_dim(x, 0, width, axis=dim)
        before = lax.ppermute(last, axis, up)
        after = lax.ppermute(initial, axis, down)
        x = jnp.concatenate([before, x, after], axis=dim)
    return x


def on_device(query, key_in, value_in, out_weight, grad_out, neighbours):
    query_rows = query[0]
    key_rows = key_in[0]
    value_rows = value_in[0]
    upstream = grad_out[0]
    tile_rows, model_cols = query_rows.shape
    head_count = model_cols // HEAD
    score_scale = 1.0 / math.sqrt(HEAD)
    tile_total = neighbours.shape[0]
    device_tile = lax.axis_index("space")
    window_tiles = device_tile - 1 + jnp.arange(3, dtype=jnp.int32)
    own_list = neighbours[device_tile]
    key_live = jnp.any(
        (own_list[None, :] == window_tiles[:, None]) & (own_list[None, :] >= 0), axis=1
    )
    inside = (window_tiles >= 0) & (window_tiles < tile_total)
    their_lists = neighbours[jnp.clip(window_tiles, 0, tile_total - 1)]
    query_live = inside & jnp.any(their_lists == device_tile, axis=1)
    key_mask = jnp.repeat(key_live, tile_rows)
    query_mask = jnp.repeat(query_live, tile_rows)
    key_value = jnp.stack([key_rows, value_rows])
    kv_near = padded(key_value, (("space", 1),), tile_rows)
    key_heads = kv_near[0].reshape(3 * tile_rows, head_count, HEAD)
    value_heads = kv_near[1].reshape(3 * tile_rows, head_count, HEAD)
    query_heads = query_rows.reshape(tile_rows, head_count, HEAD)
    scores = (
        jnp.einsum("ihd,jhd->hij", query_heads, key_heads, preferred_element_type=jnp.float32)
        * score_scale
    )
    scores = jnp.where(key_mask[None, None, :], scores, masked_score)
    row_max = jnp.max(scores, axis=2, keepdims=True)
    log_total = (row_max + jnp.log(jnp.sum(jnp.exp(scores - row_max), axis=2, keepdims=True)))[
        ..., 0
    ]
    weights = jnp.exp(scores - log_total[..., None])
    weights_bf = weights.astype(jnp.bfloat16)
    attn = (
        jnp.einsum("hij,jhd->ihd", weights_bf, value_heads, preferred_element_type=jnp.float32)
        .reshape(tile_rows, model_cols)
        .astype(jnp.bfloat16)
    )
    shard_piece = lax.all_gather(out_weight, "dp", axis=0, tiled=True)
    attn_cols = attn
    mixed_sum = jnp.dot(attn_cols, shard_piece, preferred_element_type=jnp.float32)
    new_cols = lax.dot_general(
        upstream, shard_piece, (((1,), (1,)), ((), ())), preferred_element_type=jnp.float32
    )
    back_cols = new_cols
    mixed_sum, back_cols = (mixed_sum, back_cols)
    mixed = mixed_sum.astype(jnp.bfloat16)
    grad_attn = back_cols.astype(jnp.bfloat16)
    grad_heads = grad_attn.reshape(tile_rows, head_count, HEAD)
    deltas = jnp.sum(
        grad_heads.astype(jnp.float32)
        * attn.reshape(tile_rows, head_count, HEAD).astype(jnp.float32),
        axis=2,
    ).T
    dprob = jnp.einsum("ihd,jhd->hij", grad_heads, value_heads, preferred_element_type=jnp.float32)
    dscore = (weights * (dprob - deltas[:, :, None]) * score_scale).astype(jnp.bfloat16)
    grad_query = (
        jnp.einsum("hij,jhd->ihd", dscore, key_heads, preferred_element_type=jnp.float32)
        .reshape(tile_rows, model_cols)
        .astype(jnp.bfloat16)
    )
    stat_pair = jnp.stack([log_total, deltas])
    stat_near = padded(stat_pair, (("space", 2),), tile_rows)
    query_grad = jnp.stack([query_rows, grad_attn])
    query_near = padded(query_grad, (("space", 1),), tile_rows)
    far_queries = query_near[0].reshape(3 * tile_rows, head_count, HEAD)
    far_grads = query_near[1].reshape(3 * tile_rows, head_count, HEAD)
    own_keys = key_rows.reshape(tile_rows, head_count, HEAD)
    own_values = value_rows.reshape(tile_rows, head_count, HEAD)
    back_scores = (
        jnp.einsum("jhd,ihd->hji", far_queries, own_keys, preferred_element_type=jnp.float32)
        * score_scale
    )
    back_weights = jnp.where(
        query_mask[None, :, None], jnp.exp(back_scores - stat_near[0][:, :, None]), 0.0
    )
    back_bf = back_weights.astype(jnp.bfloat16)
    grad_value = (
        jnp.einsum("hji,jhd->ihd", back_bf, far_grads, preferred_element_type=jnp.float32)
        .reshape(tile_rows, model_cols)
        .astype(jnp.bfloat16)
    )
    back_dprob = jnp.einsum(
        "jhd,ihd->hji", far_grads, own_values, preferred_element_type=jnp.float32
    )
    back_dscore = (back_weights * (back_dprob - stat_near[1][:, :, None]) * score_scale).astype(
        jnp.bfloat16
    )
    grad_key = (
        jnp.einsum("hji,jhd->ihd", back_dscore, far_queries, preferred_element_type=jnp.float32)
        .reshape(tile_rows, model_cols)
        .astype(jnp.bfloat16)
    )
    attn_cols = attn
    partial_rows = lax.psum_scatter(
        lax.dot_general(
            attn_cols, upstream, (((0,), (0,)), ((), ())), preferred_element_type=jnp.float32
        ),
        ("dp", "space"),
        scatter_dimension=0,
        tiled=True,
    )
    grad_weight = lax.all_gather(partial_rows, "space", axis=0, tiled=True)
    return (mixed[None], grad_query[None], grad_key[None], grad_value[None], grad_weight)


def solution(mesh):
    return jax.shard_map(
        on_device,
        mesh=mesh,
        in_specs=(
            P("dp", "space", None),
            P("dp", "space", None),
            P("dp", "space", None),
            P("dp", None),
            P("dp", "space", None),
            P(),
        ),
        out_specs=(
            P("dp", "space", None),
            P("dp", "space", None),
            P("dp", "space", None),
            P("dp", "space", None),
            P("dp", None),
        ),
        check_vma=False,
    )
```

profile of v0, /device:TPU:14, one launch (start us, length us, event | category | flops | bytes accessed | tf_op | source)
XLA Modules:
  0.0 448.6 jit_solution(13526817036970041660)
XLA Ops:
  7.2 0.0 copy-start
  7.2 0.0 all-gather.3.cloned.1.call-start
  7.2 0.7 all-gather.3.cloned.1.call-update
  7.9 0.0 reduce-scatter.2.cloned.1.call-start
  8.0 2.4 copy.42
  10.4 1.7 copy.41
  12.1 0.0 copy-start.10
  12.1 2.9 pad_maximum_fusion.2
  15.0 3.9 collective-permute-start.1
  18.9 1.3 collective-permute-start
  20.2 2.7 copy.43
  22.9 0.2 and_reduce_fusion
  23.1 0.1 broadcast_in_dim.45
  23.2 45.1 %collective-permute-done.1 = bf16[2,384,1536]{1,2,0:T(8,128)(2,1)} collective-permute-done((bf16[2,384,1536]{1,2,0:T(8,128)(2,1)}, bf16[2,384,1536]{1,2,0:T(8,128)(2,1)}, u32[]{:S(2)}, u32[]{:S(2)}) %collective-permute-start.1) | collective-permute-done | bytes 2359328 | tf_op jit(solution)/shard_map/ppermute | solution.py:22
  68.3 52.4 %collective-permute-done = bf16[2,384,1536]{1,2,0:T(8,128)(2,1)} collective-permute-done((bf16[2,384,1536]{1,2,0:T(8,128)(2,1)}, bf16[2,384,1536]{1,2,0:T(8,128)(2,1)}, u32[]{:S(2)}, u32[]{:S(2)}) %collective-permute-start) | collective-permute-done | bytes 2359328 | tf_op jit(solution)/shard_map/ppermute | solution.py:21
  120.7 3.6 pad_maximum_fusion
  124.3 0.0 copy-start.7
  124.3 2.3 fusion.36
  126.6 0.0 copy-done.7
  126.6 9.6 %bitcast_reduce_fusion = (f32[12,384]{1,0:T(8,128)S(1)}, f32[12,1152,384]{2,1,0:T(8,128)}) fusion(bf16[1152,12,128]{0,2,1:T(8,128)(2,1)S(1)} %bitcast.85, bf16[384,12,128]{0,2,1:T(8,128)(2,1)S(1)} %bitcast.96, pred[1152]{0:T(1024)(128)(4,1)S(1)} %broadcast_in_dim.46), kind=kOutput, calls=%fused_computation.3 | convolution fusion | flops 1374875136 | bytes 25971840 | tf_op jit(solution)/shard_map/ihd,jhd->hij/dot_general | solution.py:53
  136.2 0.0 copy-done.2
  136.2 8.8 %fusion.1 = f32[12,384]{1,0:T(8,128)S(1)} fusion(f32[12,1152,384]{2,1,0:T(8,128)} %get-tuple-element.27, f32[12,384]{1,0:T(8,128)S(1)} %get-tuple-element.26), kind=kLoop, calls=%fused_computation.5 | loop fusion | flops 10612224 | bytes 21270528 | tf_op jit(solution)/shard_map/reduce_sum | solution.py:58
  145.0 0.6 log_add_fusion
  145.6 7.5 %convolution_convert_fusion.1 = bf16[384,1536]{1,0:T(8,128)(2,1)} fusion(bf16[1536,3072]{1,0:T(8,128)(2,1)} %all-gather.3.cloned.1.call-done, bf16[1,384,3072]{2,1,0:T(8,128)(2,1)S(1)} %copy-done), kind=kOutput, calls=%fused_computation.24 | convolution fusion | flops 3624468480 | bytes 12976128 | tf_op jit(solution)/shard_map/dot_general | solution.py:71
  153.1 2.4 copy.47
  155.5 12.5 %multiply_reduce_fusion = (f32[384,12]{0,1:T(8,128)}, bf16[12,128,384]{2,1,0:T(8,128)(2,1)S(1)}) fusion(bf16[384,12,128]{0,2,1:T(8,128)(2,1)} %bitcast.94, bf16[1152,12,128]{0,2,1:T(8,128)(2,1)} %bitcast.87, f32[12,1152,384]{2,1,0:T(8,128)} %get-tuple-element.27, f32[12,384]{1,0:T(8,128)} %log_add_fusion), kind=kOutput, calls=%fused_computation.31 | convolution fusion | flops 1372515840 | bytes 27168768 | tf_op jit(solution)/shard_map/hij,jhd->ihd/dot_general | solution.py:64
  168.0 1.0 copy-done.6
  169.0 9.1 %fusion.17 = f32[1536,3072]{1,0:T(8,128)} fusion(bf16[384,1536]{0,1:T(8,128)(2,1)S(1)} %bitcast.92, bf16[1,384,3072]{2,1,0:T(8,128)(2,1)S(1)} %copy-done), kind=kOutput, calls=%fused_computation.28 | convolution fusion | flops 3623878656 | bytes 22413312 | tf_op jit(solution)/shard_map/dot_general | solution.py:125
  178.1 0.0 reduce-scatter.2.cloned.1.call-update
  178.2 0.0 all-gather.5.cloned.1.call-start
  178.2 0.6 gather_fusion
  178.8 0.1 compare_reduce_fusion
  178.9 0.1 broadcast_in_dim.50
  179.0 0.4 copy-done.3
  179.4 0.4 copy-done.5
  179.8 1.6 pad_maximum_fusion.3
  181.4 3.9 collective-permute-start.3
  185.3 1.3 collective-permute-start.2
  186.6 0.6 pad_maximum_fusion.5
  187.2 5.2 %collective-permute-start.5 = (f32[2,12,384]{2,1,0:T(8,128)}, f32[2,12,384]{2,1,0:T(8,128)}, u32[]{:S(2)}, u32[]{:S(2)}) collective-permute-start(f32[2,12,384]{2,1,0:T(8,128)} %pad_maximum_fusion.5), channel_id=1, source_target_pairs={{1,0},{2,1},{3,2},{5,4},{6,5},{7,6},{9,8},{10,9},{11,10},{13,12},{... | collective-permute-start | bytes 110600 | tf_op jit(solution)/shard_map/ppermute | solution.py:22
  192.4 1.5 collective-permute-start.4
  193.8 16.7 %fusion.20 = bf16[12,128,384]{2,1,0:T(8,128)(2,1)} fusion(bf16[1152,12,128]{0,2,1:T(8,128)(2,1)} %bitcast.86, bf16[384,12,128]{0,2,1:T(8,128)(2,1)} %bitcast.95, bf16[1152,12,128]{0,2,1:T(8,128)(2,1)} %bitcast.88, f32[12,1152,384]{2,1,0:T(8,128)} %get-tuple-element.27, f32[12,384]{1,0:T(8,128)} %bitcast.104, f32[12,384]{1,0:T(8,128)} %log_add_fusion), kind=kOutput, calls=%fused_computation.32 | convolution fusion | flops 2745040896 | bytes 30707712 | tf_op jit(solution)/shard_map/hij,jhd->ihd/dot_general | solution.py:87
  210.5 10.1 %fusion.15 = bf16[1,384,3072]{2,1,0:T(8,128)(2,1)} fusion(bf16[384,1536]{0,1:T(8,128)(2,1)} %bitcast.93, bf16[1536,3072]{1,0:T(8,128)(2,1)} %all-gather.3.cloned.1.call-done), kind=kOutput, calls=%fused_computation.23 | convolution fusion | flops 3625058304 | bytes 12976128 | tf_op jit(solution)/shard_map/dot_general | solution.py:70
  220.6 2.4 copy.60
  223.1 11.7 %collective-permute-done.5 = f32[2,12,384]{2,1,0:T(8,128)} collective-permute-done((f32[2,12,384]{2,1,0:T(8,128)}, f32[2,12,384]{2,1,0:T(8,128)}, u32[]{:S(2)}, u32[]{:S(2)}) %collective-permute-start.5) | collective-permute-done | bytes 36896 | tf_op jit(solution)/shard_map/ppermute | solution.py:22
  234.8 71.9 %collective-permute-done.4 = f32[2,12,384]{2,1,0:T(8,128)} collective-permute-done((f32[2,12,384]{2,1,0:T(8,128)}, f32[2,12,384]{2,1,0:T(8,128)}, u32[]{:S(2)}, u32[]{:S(2)}) %collective-permute-start.4) | collective-permute-done | bytes 36896 | tf_op jit(solution)/shard_map/ppermute | solution.py:21
  306.7 0.9 pad_maximum_fusion.4
  307.6 0.7 slice_bitcast_fusion.1
  308.2 0.0 collective-permute-done.3
  308.2 0.0 collective-permute-done.2
  308.3 3.4 pad_maximum_fusion.1
  311.7 3.4 fusion.35
  315.1 5.8 %copy.52 = bf16[1,1152,1536]{1,2,0:T(8,128)(2,1)} copy(bf16[1,1152,1536]{2,1,0:T(8,128)(2,1)} %get-tuple-element.21) | data formatting | bytes 7077888 | tf_op jit(solution)/shard_map/slice | solution.py:95
  320.9 5.8 %copy.56 = bf16[1,1152,1536]{1,2,0:T(8,128)(2,1)} copy(bf16[1,1152,1536]{2,1,0:T(8,128)(2,1)} %get-tuple-element.20) | data formatting | bytes 7077888 | tf_op jit(solution)/shard_map/slice | solution.py:96
  326.7 12.2 %fusion.37 = f32[12,1152,384]{2,1,0:T(8,128)} fusion(bf16[1152,12,128]{0,2,1:T(8,128)(2,1)} %bitcast.83, bf16[384,12,128]{0,2,1:T(8,128)(2,1)S(1)} %bitcast.82), kind=kOutput, calls=%fused_computation.58 | convolution fusion | flops 1358954496 | bytes 25952256 | tf_op jit(solution)/shard_map/jhd,ihd->hji/dot_general | solution.py:100
  338.9 61.5 %reduce-scatter.2.cloned.1.call-done = f32[48,3072]{1,0:T(8,128)} async-done(((f32[1536,3072]{1,0:T(8,128)}), f32[48,3072]{1,0:T(8,128)}) %reduce-scatter.2.cloned.1.call-update) | async-done | bytes 589840 | tf_op jit(solution)/shard_map/reduce_scatter | solution.py:124
  400.5 0.0 all-gather.5.cloned.1.call-update
  400.5 15.7 %fusion.21 = bf16[12,128,384]{2,1,0:T(8,128)(2,1)S(1)} fusion(bf16[1152,12,128]{0,2,1:T(8,128)(2,1)} %bitcast.84, f32[12,1152,384]{2,1,0:T(8,128)} %fusion.37, f32[12,1152]{1,0:T(8,128)} %get-tuple-element.25, f32[12,1152]{1,0:T(8,128)} %get-tuple-element.24, pred[1152]{0:T(1024)(128)(4,1)S(1)} %broadcast_in_dim.51, bf16[1152,12,128]{0,2,1:T(8,128)(2,1)} %bitcast.97, ...), kind=kOutput, calls=%fused_computation.33 | convolution fusion | flops 2755657728 | bytes 30782592 | tf_op jit(solution)/shard_map/hji,jhd->ihd/dot_general | solution.py:119
  416.2 1.5 copy.61
  417.6 11.0 %fusion.22 = bf16[12,128,384]{2,1,0:T(8,128)(2,1)S(1)} fusion(bf16[1152,12,128]{0,2,1:T(8,128)(2,1)} %bitcast.98, f32[12,1152,384]{2,1,0:T(8,128)} %fusion.37, f32[12,1152]{1,0:T(8,128)} %get-tuple-element.24, pred[1152]{0:T(1024)(128)(4,1)S(1)} %broadcast_in_dim.51), kind=kOutput, calls=%fused_computation.34 | convolution fusion | flops 1380777984 | bytes 26008704 | tf_op jit(solution)/shard_map/hji,jhd->ihd/dot_general | solution.py:108
  428.6 0.0 copy-start.1
  428.7 1.5 copy.62
  430.1 8.7 %all-gather.5.cloned.1.call-done = f32[192,3072]{1,0:T(8,128)} async-done(((f32[48,3072]{1,0:T(8,128)}), f32[192,3072]{1,0:T(8,128)}) %all-gather.5.cloned.1.call-update) | async-done | bytes 2359312 | tf_op jit(solution)/shard_map/all_gather | solution.py:132
  438.8 3.3 copy.75
  (22 shorter events, 0.1 us)
Async XLA Ops:
  7.2 138.4 %copy-start = (bf16[1,384,3072]{2,1,0:T(8,128)(2,1)S(1)}, bf16[1,384,3072]{2,1,0:T(8,128)(2,1)}, u32[]{:S(2)}) copy-start(bf16[1,384,3072]{2,1,0:T(8,128)(2,1)} %param.10) | copy-start | bytes 7077892
  7.2 138.4 %all-gather.3.cloned.1.call-start = ((), (), s32[]{:S(2)}) async-start(), calls=%async_computation.1 | async-start | bytes 10616832 | tf_op jit(solution)/shard_map/all_gather | solution.py:68
  7.9 392.5 %reduce-scatter.2.cloned.1.call-start = ((), (), s32[]{:S(2)}) async-start(), calls=%async_computation.2 | async-start | bytes 19464192 | tf_op jit(solution)/shard_map/reduce_scatter | solution.py:124
  12.1 10.8 %copy-start.10 = (s32[4,3]{1,0:T(4,128)S(1)}, s32[4,3]{1,0:T(4,128)}, u32[]{:S(2)}) copy-start(s32[4,3]{1,0:T(4,128)} %param.11) | copy-start | bytes 148
  15.0 53.2 %collective-permute-start.1 = (bf16[2,384,1536]{1,2,0:T(8,128)(2,1)}, bf16[2,384,1536]{1,2,0:T(8,128)(2,1)}, u32[]{:S(2)}, u32[]{:S(2)}) collective-permute-start(bf16[2,384,1536]{1,2,0:T(8,128)(2,1)} %pad_maximum_fusion.2), channel_id=1, source_target_pairs={{1,0},{2,1},{3,2},{5,4},{6,5},{7,6},{9,8},{10,9},{11,10},{13,12},{... | collective-permute-start | bytes 7077896 | tf_op jit(solution)/shard_map/ppermute | solution.py:22
  18.9 101.8 %collective-permute-start = (bf16[2,384,1536]{1,2,0:T(8,128)(2,1)}, bf16[2,384,1536]{1,2,0:T(8,128)(2,1)}, u32[]{:S(2)}, u32[]{:S(2)}) collective-permute-start(bf16[2,384,1536]{1,2,0:T(8,128)(2,1)} %pad_maximum_fusion.2), channel_id=1, source_target_pairs={{0,1},{1,2},{2,3},{4,5},{5,6},{6,7},{8,9},{9,10},{10,11},{12,13},{... | collective-permute-start | bytes 7077896 | tf_op jit(solution)/shard_map/ppermute | solution.py:21
  124.3 2.3 copy-start.7
  126.6 9.6 %copy-start.2 = (bf16[1,1152,1536]{1,2,0:T(8,128)(2,1)}, bf16[1,1152,1536]{1,2,0:T(8,128)(2,1)S(1)}, u32[]{:S(2)}) copy-start(bf16[1,1152,1536]{1,2,0:T(8,128)(2,1)S(1)} %get-tuple-element.22) | copy-start | bytes 10616836
  168.0 1.0 copy-start.6
  178.1 1.3 copy-start.3
  178.1 1.6 copy-start.5
  178.2 260.6 %all-gather.5.cloned.1.call-start = ((), (), s32[]{:S(2)}) async-start(), calls=%async_computation.3 | async-start | bytes 2949120 | tf_op jit(solution)/shard_map/all_gather | solution.py:132
  179.0 7.5 %copy-start.8 = (f32[12,384]{1,0:T(8,128)S(1)}, f32[12,384]{1,0:T(8,128)}, u32[]{:S(2)}) copy-start(f32[12,384]{1,0:T(8,128)} %log_add_fusion) | copy-start | bytes 55300
  179.0 7.5 %copy-start.9 = (f32[384,12]{0,1:T(8,128)S(1)}, f32[384,12]{0,1:T(8,128)}, u32[]{:S(2)}) copy-start(f32[384,12]{0,1:T(8,128)} %get-tuple-element.28) | copy-start | bytes 55300
  181.4 126.9 %collective-permute-start.3 = (bf16[2,384,1536]{2,1,0:T(8,128)(2,1)}, bf16[2,384,1536]{2,1,0:T(8,128)(2,1)}, u32[]{:S(2)}, u32[]{:S(2)}) collective-permute-start(bf16[2,384,1536]{2,1,0:T(8,128)(2,1)} %pad_maximum_fusion.3), channel_id=1, source_target_pairs={{1,0},{2,1},{3,2},{5,4},{6,5},{7,6},{9,8},{10,9},{11,10},{13,12},{... | collective-permute-start | bytes 7077896 | tf_op jit(solution)/shard_map/ppermute | solution.py:22
  185.3 123.0 %collective-permute-start.2 = (bf16[2,384,1536]{2,1,0:T(8,128)(2,1)}, bf16[2,384,1536]{2,1,0:T(8,128)(2,1)}, u32[]{:S(2)}, u32[]{:S(2)}) collective-permute-start(bf16[2,384,1536]{2,1,0:T(8,128)(2,1)} %pad_maximum_fusion.3), channel_id=1, source_target_pairs={{0,1},{1,2},{2,3},{4,5},{5,6},{6,7},{8,9},{9,10},{10,11},{12,13},{... | collective-permute-start | bytes 7077896 | tf_op jit(solution)/shard_map/ppermute | solution.py:21
  187.2 47.6 %collective-permute-start.5 = (f32[2,12,384]{2,1,0:T(8,128)}, f32[2,12,384]{2,1,0:T(8,128)}, u32[]{:S(2)}, u32[]{:S(2)}) collective-permute-start(f32[2,12,384]{2,1,0:T(8,128)} %pad_maximum_fusion.5), channel_id=1, source_target_pairs={{1,0},{2,1},{3,2},{5,4},{6,5},{7,6},{9,8},{10,9},{11,10},{13,12},{... | collective-permute-start | bytes 110600 | tf_op jit(solution)/shard_map/ppermute | solution.py:22
  192.4 114.3 %collective-permute-start.4 = (f32[2,12,384]{2,1,0:T(8,128)}, f32[2,12,384]{2,1,0:T(8,128)}, u32[]{:S(2)}, u32[]{:S(2)}) collective-permute-start(f32[2,12,384]{2,1,0:T(8,128)} %pad_maximum_fusion.5), channel_id=1, source_target_pairs={{0,1},{1,2},{2,3},{4,5},{5,6},{6,7},{8,9},{9,10},{10,11},{12,13},{... | collective-permute-start | bytes 110600 | tf_op jit(solution)/shard_map/ppermute | solution.py:21
  326.7 73.8 %copy-start.4 = (bf16[1,384,1536]{1,2,0:T(8,128)(2,1)S(1)}, bf16[1,384,1536]{1,2,0:T(8,128)(2,1)}, u32[]{:S(2)}) copy-start(bf16[1,384,1536]{1,2,0:T(8,128)(2,1)} %copy.42) | copy-start | bytes 3538948
  428.6 13.5 %copy-start.1 = (bf16[1,384,3072]{2,1,0:T(8,128)(2,1)S(1)}, bf16[1,384,3072]{2,1,0:T(8,128)(2,1)}, u32[]{:S(2)}) copy-start(bf16[1,384,3072]{2,1,0:T(8,128)(2,1)} %param.10) | copy-start | bytes 7077892
Sparse Core Ops, SparseCore 0:
  9.7 89.2 all-gather.2
  178.3 222.1 reduce-scatter.1
  402.3 36.4 all-gather.4
where the time goes:
time: 452 us; the launch traced here: 449 us
  waiting for transfers between devices  252 us (56%)
  matrix products  104 us (23%)
  local copies, waits for them, and re-layouts  38.3 us (8%)
  other arithmetic  22.8 us (5%)
  starting transfers between devices  17 us (4%)
  between operations  13.9 us (3%)
    ppermute x3, waiting for transfers between devices, padded(): before = lax.ppermute(last, axis, up)  124 us
    reduce_scatter x1, waiting for transfers between devices, on_device(): lax.psum_scatter(lax.dot_general(attn_cols, upstream, (((0,), (0,)), ((),...  61.5 us
    ppermute x3, waiting for transfers between devices, padded(): after = lax.ppermute(initial, axis, down)  56.9 us
    unnamed x29, local copies, waits for them, and re-layouts  17.1 us
    dot_general x1, matrix products, on_device(): jnp.einsum('hij,jhd->ihd', dscore, key_heads, preferred_element_type=jnp....  16.7 us
    dot_general x1, matrix products, on_device(): jnp.einsum('hji,jhd->ihd', back_dscore, far_queries, preferred_element_ty...  15.7 us
    ppermute x3, starting transfers between devices, padded(): after = lax.ppermute(initial, axis, down)  12.9 us
    dot_general x1, matrix products, on_device(): jnp.einsum('hij,jhd->ihd', weights_bf, value_heads, preferred_element_typ...  12.5 us
  transfers between devices with their start and end apart: 9, of which 6 were waited for; matrix products, arithmetic and copies ran while one was open for 29% of the time, Pallas kernels for 0%

commit v1 on v0

--- a/solution.py
+++ b/solution.py
@@ -1,8 +1,11 @@
+import functools
 import math
 
 import jax
 import jax.numpy as jnp
 from jax import lax
+from jax.experimental import pallas as pl
+from jax.experimental.pallas import tpu as pltpu
 from jax.sharding import PartitionSpec as P
 
 HEAD = 128
@@ -24,7 +27,7 @@
     return x
 
 
-def on_device(query, key_in, value_in, out_weight, grad_out, neighbours):
+def halo_on_device(query, key_in, value_in, out_weight, grad_out, neighbours):
     query_rows = query[0]
     key_rows = key_in[0]
     value_rows = value_in[0]
@@ -133,7 +136,282 @@
     return (mixed[None], grad_query[None], grad_key[None], grad_value[None], grad_weight)
 
 
+MESH = pl.DeviceIdType.MESH
+SCALE = 1.0 / math.sqrt(HEAD)
+
+
+def window(tile, tiles):
+    return range(max(0, tile - 1), min(tiles, tile + 2))
+
+
+def tile_bias(near, tile, other):
+    live = near[tile, 0] == other
+    for slot in range(1, near.shape[1]):
+        live = jnp.logical_or(live, near[tile, slot] == other)
+    return jnp.where(live, 0.0, masked_score).astype(jnp.float32)
+
+
+def dot_nt(a, b):
+    return lax.dot_general(a, b, (((1,), (1,)), ((), ())), preferred_element_type=jnp.float32)
+
+
+def dot_tn(a, b):
+    return lax.dot_general(a, b, (((0,), (0,)), ((), ())), preferred_element_type=jnp.float32)
+
+
+def greet(n):
+    me = lax.axis_index("space")
+    barrier = pltpu.get_barrier_semaphore()
+    for off in range(1, n):
+        pl.semaphore_signal(
+            barrier, inc=1, device_id={"space": lax.rem(me + off, n)}, device_id_type=MESH
+        )
+    pl.semaphore_wait(barrier, n - 1)
+
+
+def send(src, dst, send_sem, recv_sem, peer):
+    return pltpu.make_async_remote_copy(
+        src_ref=src,
+        dst_ref=dst,
+        send_sem=send_sem,
+        recv_sem=recv_sem,
+        device_id={"space": peer},
+        device_id_type=MESH,
+    )
+
+
+def to_heads(n, pairs, send_sem, recv_sem, own_sem):
+    me = lax.axis_index("space")
+    rows, width = pairs[0][0].shape[0], pairs[0][1].shape[1]
+    mine = pl.ds(pl.multiple_of(me * rows, rows), rows)
+    copies = []
+    for off in range(1, n):
+        peer = lax.rem(me + off, n)
+        cols = pl.ds(pl.multiple_of(peer * width, width), width)
+        for a, (src, dst) in enumerate(pairs):
+            copy = send(
+                src.at[:, cols], dst.at[mine], send_sem.at[a, off], recv_sem.at[a, off], peer
+            )
+            copy.start()
+            copies.append(copy)
+    cols = pl.ds(pl.multiple_of(me * width, width), width)
+    for a, (src, dst) in enumerate(pairs):
+        copy = pltpu.make_async_copy(src.at[:, cols], dst.at[mine], own_sem.at[a])
+        copy.start()
+        copies.append(copy)
+    return copies
+
+
+def forward_kernel(
+    n, near, q, k, v, attn, qh, kh, vh, ah, log_total, send_sem, recv_sem, own_sem,
+    back_send, back_recv, back_own,
+):
+    me = lax.axis_index("space")
+    rows = q.shape[0]
+    width = qh.shape[1]
+    greet(n)
+    for copy in to_heads(n, ((q, qh), (k, kh), (v, vh)), send_sem, recv_sem, own_sem):
+        copy.wait()
+    my_cols = pl.ds(pl.multiple_of(me * width, width), width)
+    for t in range(n):
+        here = pl.ds(t * rows, rows)
+        biases = [tile_bias(near, t, u) for u in window(t, n)]
+
+        def one_head(h, carry):
+            cols = pl.ds(pl.multiple_of(h * HEAD, HEAD), HEAD)
+            query = qh[here, cols]
+            scores = [
+                dot_nt(query, kh[pl.ds(u * rows, rows), cols]) * SCALE + bias
+                for u, bias in zip(window(t, n), biases)
+            ]
+            top = functools.reduce(
+                jnp.maximum, [jnp.max(s, axis=1, keepdims=True) for s in scores]
+            )
+            parts = [jnp.exp(s - top) for s in scores]
+            total = sum(jnp.sum(p, axis=1, keepdims=True) for p in parts)
+            mixed = sum(
+                jnp.dot(
+                    p.astype(jnp.bfloat16),
+                    vh[pl.ds(u * rows, rows), cols],
+                    preferred_element_type=jnp.float32,
+                )
+                for u, p in zip(window(t, n), parts)
+            )
+            ah[here, cols] = (mixed / total).astype(jnp.bfloat16)
+            log_total[h, here, :] = top + jnp.log(total)
+            return carry
+
+        lax.fori_loop(0, width // HEAD, one_head, 0)
+
+        @pl.when(me != t)
+        def _():
+            send(ah.at[here], attn.at[:, my_cols], back_send.at[t], back_recv.at[me], t).start()
+
+        @pl.when(me == t)
+        def _():
+            pltpu.make_async_copy(ah.at[here], attn.at[:, my_cols], back_own).start()
+
+    for off in range(1, n):
+        peer = lax.rem(me + off, n)
+        their = pl.ds(pl.multiple_of(peer * rows, rows), rows)
+        their_cols = pl.ds(pl.multiple_of(peer * width, width), width)
+        send(ah.at[their], attn.at[:, my_cols], back_send.at[peer], back_recv.at[me], peer).wait_send()
+        send(
+            ah.at[their], attn.at[:, their_cols], back_send.at[peer], back_recv.at[peer], peer
+        ).wait_recv()
+    mine = pl.ds(pl.multiple_of(me * rows, rows), rows)
+    pltpu.make_async_copy(ah.at[mine], attn.at[:, my_cols], back_own).wait()
+
+
+def backward_kernel(
+    n, near, ga, qh, kh, vh, ah, log_total, dq, dk, dv, gh, dqh, dkh, dvh, dk_sum, dv_sum,
+    send_sem, recv_sem, own_sem, back_send, back_recv, back_own,
+):
+    me = lax.axis_index("space")
+    rows = ga.shape[0]
+    width = qh.shape[1]
+    greet(n)
+    copies = to_heads(n, ((ga, gh),), send_sem, recv_sem, own_sem)
+    dk_sum[...] = jnp.zeros_like(dk_sum)
+    dv_sum[...] = jnp.zeros_like(dv_sum)
+    for copy in copies:
+        copy.wait()
+    my_cols = pl.ds(pl.multiple_of(me * width, width), width)
+
+    def give(a, src, dst, t):
+        here = pl.ds(t * rows, rows)
+
+        @pl.when(me != t)
+        def _():
+            send(
+                src.at[here], dst.at[:, my_cols], back_send.at[a, t], back_recv.at[a, me], t
+            ).start()
+
+        @pl.when(me == t)
+        def _():
+            pltpu.make_async_copy(src.at[here], dst.at[:, my_cols], back_own.at[a]).start()
+
+    def give_key(t):
+        here = pl.ds(t * rows, rows)
+        dkh[here, :] = dk_sum[here, :].astype(jnp.bfloat16)
+        dvh[here, :] = dv_sum[here, :].astype(jnp.bfloat16)
+        give(1, dkh, dk, t)
+        give(2, dvh, dv, t)
+
+    for t in range(n):
+        here = pl.ds(t * rows, rows)
+        biases = [tile_bias(near, t, u) for u in window(t, n)]
+
+        def one_head(h, carry):
+            cols = pl.ds(pl.multiple_of(h * HEAD, HEAD), HEAD)
+            query, grad = qh[here, cols], gh[here, cols]
+            level = log_total[h, here, :]
+            delta = jnp.sum(
+                grad.astype(jnp.float32) * ah[here, cols].astype(jnp.float32),
+                axis=1,
+                keepdims=True,
+            )
+            out = jnp.zeros((rows, HEAD), jnp.float32)
+            for u, bias in zip(window(t, n), biases):
+                there = pl.ds(u * rows, rows)
+                key, value = kh[there, cols], vh[there, cols]
+                weight = jnp.exp(dot_nt(query, key) * SCALE + bias - level)
+                dscore = (weight * (dot_nt(grad, value) - delta) * SCALE).astype(jnp.bfloat16)
+                out += jnp.dot(dscore, key, preferred_element_type=jnp.float32)
+                dk_sum[there, cols] += dot_tn(dscore, query)
+                dv_sum[there, cols] += dot_tn(weight.astype(jnp.bfloat16), grad)
+            dqh[here, cols] = out.astype(jnp.bfloat16)
+            return carry
+
+        lax.fori_loop(0, width // HEAD, one_head, 0)
+        give(0, dqh, dq, t)
+        if t >= 1:
+            give_key(t - 1)
+    give_key(n - 1)
+    mine = pl.ds(pl.multiple_of(me * rows, rows), rows)
+    for a, (src, dst) in enumerate(((dqh, dq), (dkh, dk), (dvh, dv))):
+        for off in range(1, n):
+            peer = lax.rem(me + off, n)
+            their = pl.ds(pl.multiple_of(peer * rows, rows), rows)
+            their_cols = pl.ds(pl.multiple_of(peer * width, width), width)
+            send(
+                src.at[their], dst.at[:, my_cols], back_send.at[a, peer], back_recv.at[a, me], peer
+            ).wait_send()
+            send(
+                src.at[their],
+                dst.at[:, their_cols],
+                back_send.at[a, peer],
+                back_recv.at[a, peer],
+                peer,
+            ).wait_recv()
+        pltpu.make_async_copy(src.at[mine], dst.at[:, my_cols], back_own.at[a]).wait()
+
+
+def sems(*shape):
+    return pltpu.SemaphoreType.DMA(shape)
+
+
+def heads_on_device(n, query, key_in, value_in, out_weight, grad_out, neighbours):
+    upstream = grad_out[0]
+    rows, model_cols = query.shape[1:]
+    width = model_cols // n
+    heads = width // HEAD
+    bf16, f32 = jnp.bfloat16, jnp.float32
+    weight = lax.all_gather(out_weight, "dp", axis=0, tiled=True)
+    hbm = pl.BlockSpec(memory_space=pl.ANY)
+    vmem = pl.BlockSpec(memory_space=pltpu.VMEM)
+    smem = pl.BlockSpec(memory_space=pltpu.SMEM)
+    wide = jax.ShapeDtypeStruct((rows, model_cols), bf16)
+    tall = jax.ShapeDtypeStruct((n * rows, width), bf16)
+    level = jax.ShapeDtypeStruct((heads, n * rows, 1), f32)
+    attn, qh, kh, vh, ah, log_total = pl.pallas_call(
+        functools.partial(forward_kernel, n),
+        out_shape=(wide, tall, tall, tall, tall, level),
+        in_specs=[smem, hbm, hbm, hbm],
+        out_specs=(hbm, vmem, vmem, vmem, vmem, vmem),
+        scratch_shapes=[
+            sems(3, n), sems(3, n), sems(3), sems(n), sems(n), pltpu.SemaphoreType.DMA,
+        ],
+        compiler_params=pltpu.CompilerParams(
+            collective_id=0, has_side_effects=True, vmem_limit_bytes=50 * 2**20
+        ),
+        name="attend",
+    )(neighbours, query[0], key_in[0], value_in[0])
+    partial_weight = dot_tn(attn, upstream).astype(bf16)
+    piece = lax.psum_scatter(partial_weight, ("dp", "space"), scatter_dimension=0, tiled=True)
+    grad_attn = dot_nt(upstream, weight).astype(bf16)
+    dq, dk, dv = pl.pallas_call(
+        functools.partial(backward_kernel, n),
+        out_shape=(wide, wide, wide),
+        in_specs=[smem, hbm, vmem, vmem, vmem, vmem, vmem],
+        out_specs=(hbm, hbm, hbm),
+        scratch_shapes=[
+            pltpu.VMEM(tall.shape, bf16),
+            pltpu.VMEM(tall.shape, bf16),
+            pltpu.VMEM(tall.shape, bf16),
+            pltpu.VMEM(tall.shape, bf16),
+            pltpu.VMEM(tall.shape, f32),
+            pltpu.VMEM(tall.shape, f32),
+            sems(1, n), sems(1, n), sems(1), sems(3, n), sems(3, n), sems(3),
+        ],
+        compiler_params=pltpu.CompilerParams(
+            collective_id=1, has_side_effects=True, vmem_limit_bytes=50 * 2**20
+        ),
+        name="attend_back",
+    )(neighbours, grad_attn, qh, kh, vh, ah, log_total)
+    mixed = jnp.dot(attn, weight, preferred_element_type=f32).astype(bf16)
+    grad_weight = lax.all_gather(piece, "space", axis=0, tiled=True).astype(f32)
+    return (mixed[None], dq[None], dk[None], dv[None], grad_weight)
+
+
 def solution(mesh):
+    n = mesh.shape["space"]
+
+    def on_device(query, *rest):
+        if query.shape[2] % (n * HEAD) == 0:
+            return heads_on_device(n, query, *rest)
+        return halo_on_device(query, *rest)
+
     return jax.shard_map(
         on_device,
         mesh=mesh,

time: 452 us -> 448 us (level)
  Pallas kernels: 0 us -> 146 us
  matrix products: 104 us -> 24 us
  local copies, waits for them, and re-layouts: 38.3 us -> 5.9 us
  other arithmetic: 22.8 us -> 2.93 us
  starting transfers between devices: 17 us -> 0.12 us
    ppermute x6 -> x0, waiting for transfers between devices: 181 us -> none  [the longest x3 124 us: padded(): before = lax.ppermute(last, axis, up)]
    pallas_call x0 -> x2, Pallas kernels: none -> 146 us  [the longest x1 78.2 us: heads_on_device(): pl.pallas_call(functools.partial(backward_kernel, n), out_shape=(wide, wi...]
    all_gather x2, waiting for transfers between devices: 8.7 us -> 115 us  [the longest x1 88 us: heads_on_device(): weight = lax.all_gather(out_weight, 'dp', axis=0, tiled=True)]
    dot_general x9 -> x3, matrix products: 104 us -> 24 us  [the longest x1 8.73 us: heads_on_device(): mixed = jnp.dot(attn, weight, preferred_element_type=f32).astype(bf16)]
    reduce_scatter x1, waiting for transfers between devices: 61.5 us -> 136 us  [heads_on_device(): lax.psum_scatter(partial_weight, ('dp', 'space'), scatter_dimension=0, ti...]
    slice x4 -> x0, local copies, waits for them, and re-layouts: 17.3 us -> none  [the longest x2 9.21 us: on_device(): far_grads = query_near[1].reshape(3 * tile_rows, head_count, HEAD)]
    ppermute x6 -> x0, starting transfers between devices: 16.9 us -> none  [the longest x3 12.9 us: padded(): after = lax.ppermute(initial, axis, down)]
    unnamed x29 -> x13, local copies, waits for them, and re-layouts: 17.1 us -> 5.9 us
  transfers between devices with their start and end apart: 9 -> 3, of which waited for: 6 -> 3; matrix products, arithmetic and copies ran while one was open for 29% -> 1% of each run, Pallas kernels for 0% -> 0%
where the time goes in v1:
time: 448 us; the launch traced here: 445 us
  waiting for transfers between devices  253 us (56%)
  Pallas kernels  146 us (33%)
  matrix products  24 us (5%)
  between operations  13.8 us (3%)
  local copies, waits for them, and re-layouts  5.9 us (1%)
    reduce_scatter x1, waiting for transfers between devices, heads_on_device(): lax.psum_scatter(partial_weight, ('dp', 'space'), scatter_dimension=0, ti...  136 us
    all_gather x1, waiting for transfers between devices, heads_on_device(): weight = lax.all_gather(out_weight, 'dp', axis=0, tiled=True)  88 us
    pallas_call x1, Pallas kernels, heads_on_device(): pl.pallas_call(functools.partial(backward_kernel, n), out_shape=(wide, wi...  78.2 us
    pallas_call x1, Pallas kernels, heads_on_device(): pl.pallas_call(functools.partial(forward_kernel, n), out_shape=(wide, tal...  67.4 us
    all_gather x1, waiting for transfers between devices, heads_on_device(): grad_weight = lax.all_gather(piece, 'space', axis=0, tiled=True).astype(f32)  27.4 us
  transfers between devices with their start and end apart: 3, of which 3 were waited for; matrix products, arithmetic and copies ran while one was open for 1% of the time, Pallas kernels for 0%

profile of v1, /device:TPU:14, one launch (start us, length us, event | category | flops | bytes accessed | tf_op | source)
XLA Modules:
  0.0 444.9 jit_solution(14187122159282584283)
XLA Ops:
  7.2 0.0 copy-start
  7.2 0.0 reduce-scatter.2.cloned.1.call-start
  7.2 0.0 copy-start.3
  7.2 0.8 copy-done.3
  8.1 67.4 %attend.1 = (bf16[384,1536]{1,0:T(8,128)(2,1)S(1)}, bf16[1536,384]{1,0:T(8,128)(2,1)S(1)}, bf16[1536,384]{1,0:T(8,128)(2,1)S(1)}, bf16[1536,384]{1,0:T(8,128)(2,...) custom-call(s32[4,3]{1,0:T(4,128)S(1)} %copy-done.3, bf16[384,1536]{1,0:T(8,128)(2,1)} %bitcast.20, ...), custom_call_target="tpu_custom_call" | custom-call | tf_op jit(solution)/shard_map/attend/pallas_call | solution.py:367
  75.5 0.0 copy-start.1
  75.5 1.0 copy-done.1
  76.5 0.0 copy-start.2
  76.5 1.0 copy-done.2
  77.5 0.0 copy-done
  77.5 7.8 %convolution_convert_fusion = bf16[1536,3072]{1,0:T(8,128)(2,1)} fusion(bf16[384,1536]{1,0:T(8,128)(2,1)S(1)} %get-tuple-element.14, bf16[1,384,3072]{2,1,0:T(8,128)(2,1)S(1)} %copy-done), kind=kOutput, calls=%fused_computation | convolution fusion | flops 3628597248 | bytes 12976128 | tf_op jit(solution)/shard_map/dot_general | solution.py:159
  85.3 0.0 reduce-scatter.2.cloned.1.call-update
  85.3 0.0 all-gather.5.cloned.1.call-start
  85.3 136.5 %reduce-scatter.2.cloned.1.call-done = bf16[48,3072]{1,0:T(8,128)(2,1)} async-done(((bf16[1536,3072]{1,0:T(8,128)(2,1)}), bf16[48,3072]{1,0:T(8,128)(2,1)}) %reduce-scatter.2.cloned.1.call-update) | async-done | bytes 294928 | tf_op jit(solution)/shard_map/reduce_scatter | solution.py:381
  221.8 0.0 all-gather.5.cloned.1.call-update
  221.8 0.0 all-gather.3.cloned.1.call-start
  221.9 0.7 all-gather.3.cloned.1.call-update
  222.6 27.4 %all-gather.5.cloned.1.call-done = bf16[192,3072]{1,0:T(8,128)(2,1)} async-done(((bf16[48,3072]{1,0:T(8,128)(2,1)}), bf16[192,3072]{1,0:T(8,128)(2,1)}) %all-gather.5.cloned.1.call-update) | async-done | bytes 1179664 | tf_op jit(solution)/shard_map/all_gather | solution.py:403
  249.9 2.9 convert_element_type.15
  252.9 0.0 copy-start.4
  252.9 88.0 %all-gather.3.cloned.1.call-done = bf16[1536,3072]{1,0:T(8,128)(2,1)} async-done(((bf16[192,3072]{1,0:T(8,128)(2,1)}), bf16[1536,3072]{1,0:T(8,128)(2,1)}) %all-gather.3.cloned.1.call-update) | async-done | bytes 9437200 | tf_op jit(solution)/shard_map/all_gather | solution.py:360
  340.8 7.5 %convolution_convert_fusion.2.ga = bf16[384,1536]{1,0:T(8,128)(2,1)} fusion(bf16[1536,3072]{1,0:T(8,128)(2,1)} %all-gather.3.cloned.1.call-done, bf16[1,384,3072]{2,1,0:T(8,128)(2,1)S(1)} %copy-done), kind=kOutput, calls=%fused_computation.3 | convolution fusion | flops 3624468480 | bytes 12976128 | tf_op jit(solution)/shard_map/dot_general | solution.py:155
  348.4 0.0 copy-done.4
  348.4 78.2 %attend_back.1 = (bf16[384,1536]{1,0:T(8,128)(2,1)S(1)}, bf16[384,1536]{1,0:T(8,128)(2,1)S(1)}, bf16[384,1536]{1,0:T(8,128)(2,1)S(1)}) custom-call(s32[4,3]{1,0:T(4,128)S(1)} %copy-done.4, bf16[384,1536]{1,0:T(8,128)(2,1)} %convolution_convert_fusion.2.ga, bf16[1536,384]{1,0:T(8,128)(2,1)} %copy-done.1, bf16[1536,384]{1,0:T(8,128)(2,1)} %copy-done.2, ...), custom_call_target="tpu_custom_call" | custom-call | tf_op jit(solution)/shard_map/attend_back/pallas_call | solution.py:383
  426.6 8.7 %fusion = bf16[1,384,3072]{2,1,0:T(8,128)(2,1)} fusion(bf16[384,1536]{1,0:T(8,128)(2,1)S(1)} %get-tuple-element.14, bf16[1536,3072]{1,0:T(8,128)(2,1)} %all-gather.3.cloned.1.call-done), kind=kOutput, calls=%fused_computation.2 | convolution fusion | flops 3625058304 | bytes 12976128 | tf_op jit(solution)/shard_map/dot_general | solution.py:402
  435.3 1.0 copy.14
  436.3 1.0 copy.15
  437.3 1.0 copy.16
Async XLA Ops:
  7.2 70.3 %copy-start = (bf16[1,384,3072]{2,1,0:T(8,128)(2,1)S(1)}, bf16[1,384,3072]{2,1,0:T(8,128)(2,1)}, u32[]{:S(2)}) copy-start(bf16[1,384,3072]{2,1,0:T(8,128)(2,1)} %param.10) | copy-start | bytes 7077892
  7.2 214.6 %reduce-scatter.2.cloned.1.call-start = ((), (), s32[]{:S(2)}) async-start(), calls=%async_computation.2 | async-start | bytes 9732096 | tf_op jit(solution)/shard_map/reduce_scatter | solution.py:381
  7.2 0.8 copy-start.3
  75.5 1.0 copy-start.1
  76.5 1.0 copy-start.2
  85.3 164.7 %all-gather.5.cloned.1.call-start = ((), (), s32[]{:S(2)}) async-start(), calls=%async_computation.3 | async-start | bytes 1474560 | tf_op jit(solution)/shard_map/all_gather | solution.py:403
  221.8 119.0 %all-gather.3.cloned.1.call-start = ((), (), s32[]{:S(2)}) async-start(), calls=%async_computation.1 | async-start | bytes 10616832 | tf_op jit(solution)/shard_map/all_gather | solution.py:360
  252.9 95.5 %copy-start.4 = (s32[4,3]{1,0:T(4,128)S(1)}, s32[4,3]{1,0:T(4,128)}, u32[]{:S(2)}) copy-start(s32[4,3]{1,0:T(4,128)} %near.3) | copy-start | bytes 148
Sparse Core Ops, SparseCore 0:
  85.4 136.3 reduce-scatter.1
  223.8 26.1 all-gather.4
  251.7 89.1 all-gather.2

commit v2 on v1

--- a/solution.py
+++ b/solution.py
@@ -159,25 +159,37 @@
     return lax.dot_general(a, b, (((0,), (0,)), ((), ())), preferred_element_type=jnp.float32)
 
 
-def greet(n):
-    me = lax.axis_index("space")
+def place(nz):
+    row = lax.axis_index("dp")
+    return row // 2, row % 2, lax.axis_index("space")
+
+
+def greet(peers):
     barrier = pltpu.get_barrier_semaphore()
-    for off in range(1, n):
+    for row, column in peers:
         pl.semaphore_signal(
-            barrier, inc=1, device_id={"space": lax.rem(me + off, n)}, device_id_type=MESH
+            barrier, inc=1, device_id={"dp": row, "space": column}, device_id_type=MESH
         )
-    pl.semaphore_wait(barrier, n - 1)
-
-
-def send(src, dst, send_sem, recv_sem, peer):
+    pl.semaphore_wait(barrier, len(peers))
+
+
+def send_to(src, dst, send_sem, recv_sem, row, column):
     return pltpu.make_async_remote_copy(
         src_ref=src,
         dst_ref=dst,
         send_sem=send_sem,
         recv_sem=recv_sem,
-        device_id={"space": peer},
+        device_id={"dp": row, "space": column},
         device_id_type=MESH,
     )
+
+
+def send(src, dst, send_sem, recv_sem, peer):
+    return send_to(src, dst, send_sem, recv_sem, lax.axis_index("dp"), peer)
+
+
+def block(index, size):
+    return pl.ds(pl.multiple_of(index * size, size), size)
 
 
 def to_heads(n, pairs, send_sem, recv_sem, own_sem):
@@ -203,15 +215,80 @@
 
 
 def forward_kernel(
-    n, near, q, k, v, attn, qh, kh, vh, ah, log_total, send_sem, recv_sem, own_sem,
-    back_send, back_recv, back_own,
+    n, nz, near, q, k, v, g, w, attn, attn_other, g_other, wf, qh, kh, vh, ah, log_total,
+    send_sem, recv_sem, own_sem, back_send, back_recv, back_own,
+    core_send, core_recv, zq_send, zq_recv, zh_send, zh_recv, sq_send, sq_recv,
+    cq_send, cq_recv, ch_send, ch_recv,
 ):
-    me = lax.axis_index("space")
+    z, core, me = place(nz)
+    mine_dp = 2 * z + core
+    twin = 2 * z + 1 - core
     rows = q.shape[0]
     width = qh.shape[1]
-    greet(n)
-    for copy in to_heads(n, ((q, qh), (k, kh), (v, vh)), send_sem, recv_sem, own_sem):
+    depth, model = w.shape
+    half = model // 2
+    quarter = half // n
+    upper = pl.ds(half, half)
+    greet(
+        [(mine_dp, lax.rem(me + o, n)) for o in range(1, n)]
+        + [(2 * lax.rem(z + o, nz) + core, me) for o in range(1, nz)]
+        + [(twin, me)]
+    )
+    shard = block(mine_dp, depth)
+    my_quarter = block(me, quarter)
+    done = []
+
+    def begin(copy):
+        copy.start()
+        done.append(copy)
+
+    token_copies = to_heads(n, ((q, qh), (k, kh), (v, vh)), send_sem, recv_sem, own_sem)
+    from_z, halves = [], []
+    for o in range(1, nz):
+        peer = 2 * lax.rem(z + o, nz) + core
+        copy = send_to(
+            w.at[:, my_quarter], wf.at[shard, my_quarter], zq_send.at[o], zq_recv.at[o], peer, me
+        )
+        copy.start()
+        from_z.append(copy)
+    for o in range(1, nz):
+        peer = 2 * lax.rem(z + o, nz) + core
+        copy = send_to(w.at[:, upper], wf.at[shard, upper], zh_send.at[o], zh_recv.at[o], peer, me)
+        copy.start()
+        halves.append(copy)
+    begin(pltpu.make_async_copy(w, wf.at[shard], own_sem.at[3]))
+    begin(send_to(w, wf.at[shard], core_send.at[0], core_recv.at[0], twin, me))
+    begin(
+        send_to(
+            g.at[:, block(1 - core, half)], g_other, core_send.at[1], core_recv.at[1], twin, me
+        )
+    )
+    for copy in token_copies:
         copy.wait()
+    quarters = []
+    for o in range(1, nz):
+        from_z[o - 1].wait()
+        theirs = block(2 * lax.rem(z + nz - o, nz) + core, depth)
+        part = wf.at[theirs, my_quarter]
+        for p in range(1, n):
+            copy = send(part, part, sq_send.at[o, p], sq_recv.at[o, p], lax.rem(me + p, n))
+            copy.start()
+            quarters.append((o, p, copy))
+        begin(send_to(part, part, cq_send.at[o, 0], cq_recv.at[o, 0], twin, me))
+
+    def pass_halves():
+        for o in range(1, nz):
+            halves[o - 1].wait()
+            part = wf.at[block(2 * lax.rem(z + nz - o, nz) + core, depth), upper]
+            begin(send_to(part, part, ch_send.at[o], ch_recv.at[o], twin, me))
+
+    def pass_quarters():
+        for o, p, copy in quarters:
+            copy.wait()
+            theirs = block(2 * lax.rem(z + nz - o, nz) + core, depth)
+            part = wf.at[theirs, block(lax.rem(me + n - p, n), quarter)]
+            begin(send_to(part, part, cq_send.at[o, p], cq_recv.at[o, p], twin, me))
+
     my_cols = pl.ds(pl.multiple_of(me * width, width), width)
     for t in range(n):
         here = pl.ds(t * rows, rows)
@@ -261,19 +338,156 @@
         ).wait_recv()
     mine = pl.ds(pl.multiple_of(me * rows, rows), rows)
     pltpu.make_async_copy(ah.at[mine], attn.at[:, my_cols], back_own).wait()
+    begin(send_to(attn, attn_other, core_send.at[2], core_recv.at[2], twin, me))
+    pass_quarters()
+    pass_halves()
+    for copy in done:
+        copy.wait()
 
 
 def backward_kernel(
-    n, near, ga, qh, kh, vh, ah, log_total, dq, dk, dv, gh, dqh, dkh, dvh, dk_sum, dv_sum,
+    n, nz, near, ga, qh, kh, vh, ah, log_total, attn, attn_other, g, g_other, wf,
+    dq, dk, dv, gw, mixed, gh, dqh, dkh, dvh, dk_sum, dv_sum,
+    wv, gv, px, pz, xin, x_sum, xzin, zin, z_sum, zxin, total,
     send_sem, recv_sem, own_sem, back_send, back_recv, back_own,
+    w_sem, xs, xr, xzs, xzr, zs, zr, zxs, zxr, fs, fr, f_own,
 ):
-    me = lax.axis_index("space")
+    z, core, me = place(nz)
+    mine_dp = 2 * z + core
     rows = ga.shape[0]
     width = qh.shape[1]
-    greet(n)
+    half = gv.shape[1]
+    split = px.shape[3]
+    piece = px.shape[2]
+    per = n // 2
+    heir = 2 * z + me // per
+    greet(
+        [(mine_dp, lax.rem(me + o, n)) for o in range(1, n)]
+        + [(2 * lax.rem(z + o, nz) + core, me) for o in range(1, nz)]
+        + [(2 * z + 1 - core, lax.rem(me + o, n)) for o in range(n)]
+    )
     copies = to_heads(n, ((ga, gh),), send_sem, recv_sem, own_sem)
+    load_g = pltpu.make_async_copy(g.at[:, block(core, half)], gv, w_sem.at[1])
+    load_g.start()
+    load_w = pltpu.make_async_copy(wf, wv, w_sem.at[0])
+    load_w.start()
     dk_sum[...] = jnp.zeros_like(dk_sum)
     dv_sum[...] = jnp.zeros_like(dv_sum)
+    load_g.wait()
+    z_copies = [
+        send_to(
+            pz.at[lax.rem(z + o, nz)], zin.at[o], zs.at[o], zr.at[o],
+            2 * lax.rem(z + o, nz) + core, me,
+        )
+        for o in range(1, nz)
+    ]
+    x_copies = [
+        send(px.at[:, lax.rem(me + o, n)], xin.at[o], xs.at[o], xr.at[o], lax.rem(me + o, n))
+        for o in range(1, n)
+    ]
+
+    def product(i, start):
+        cols = block(i, n * piece)
+        part = pl.ds(start, split)
+        return dot_tn(attn[:, cols], gv[:, part]) + dot_tn(attn_other[:, cols], g_other[:, part])
+
+    def z_part(i, carry):
+        pz[i] = product(i, split).astype(jnp.bfloat16).reshape(pz.shape[1:])
+        return carry
+
+    def x_part(i, carry):
+        px[i] = product(i, 0).astype(jnp.bfloat16).reshape(px.shape[1:])
+        return carry
+
+    lax.fori_loop(0, nz, z_part, 0)
+    for copy in z_copies:
+        copy.start()
+    lax.fori_loop(0, nz, x_part, 0)
+    for copy in x_copies:
+        copy.start()
+
+    def wide(ref):
+        return ref.astype(jnp.float32)
+
+    xz_copies = [
+        send_to(
+            x_sum.at[lax.rem(z + o, nz)], xzin.at[o], xzs.at[o], xzr.at[o],
+            2 * lax.rem(z + o, nz) + core, me,
+        )
+        for o in range(1, nz)
+    ]
+    zx_copies = [
+        send(z_sum.at[lax.rem(me + o, n)], zxin.at[o], zxs.at[o], zxr.at[o], lax.rem(me + o, n))
+        for o in range(1, n)
+    ]
+
+    def add_x():
+        for copy in x_copies:
+            copy.wait()
+        for i in range(nz):
+            x_sum[i] = (
+                wide(px[i, me]) + sum(wide(xin[o, i]) for o in range(1, n))
+            ).astype(jnp.bfloat16)
+        for copy in xz_copies:
+            copy.start()
+
+    def add_z():
+        for copy in z_copies:
+            copy.wait()
+        for i in range(n):
+            z_sum[i] = (
+                wide(pz[z, i]) + sum(wide(zin[o, i]) for o in range(1, nz))
+            ).astype(jnp.bfloat16)
+        for copy in zx_copies:
+            copy.start()
+
+    my_part = gw.at[block(lax.rem(me, per), piece), block(core, half)]
+
+    def shares(start):
+        for o in range(n):
+            column = lax.rem(me + o, n)
+            slot = core * n + me
+
+            def remote():
+                copy = send_to(total, my_part, fs.at[o], fr.at[slot], heir, column)
+                copy.start() if start else copy.wait_send()
+
+            def local():
+                copy = pltpu.make_async_copy(total, my_part, f_own)
+                copy.start() if start else copy.wait()
+
+            if o > 0:
+                remote()
+            else:
+                pl.when(heir != mine_dp)(remote)
+                pl.when(heir == mine_dp)(local)
+
+    def add_last():
+        for copy in xz_copies:
+            copy.wait()
+        for copy in zx_copies:
+            copy.wait()
+        total[:, pl.ds(0, split)] = (
+            wide(x_sum[z]) + sum(wide(xzin[o]) for o in range(1, nz))
+        ).astype(jnp.bfloat16)
+        total[:, pl.ds(split, split)] = (
+            wide(z_sum[me]) + sum(wide(zxin[o]) for o in range(1, n))
+        ).astype(jnp.bfloat16)
+        shares(True)
+
+    def take_shares():
+        shares(False)
+        for c in range(2):
+            for j in range(per):
+                source = core * per + j
+                part = gw.at[pl.ds(j * piece, piece), pl.ds(c * half, half)]
+
+                @pl.when(jnp.logical_or(source != me, core != c))
+                def _():
+                    send_to(
+                        total, part, fs.at[0], fr.at[c * n + source], 2 * z + 1 - core, me
+                    ).wait_recv()
+
     for copy in copies:
         copy.wait()
     my_cols = pl.ds(pl.multiple_of(me * width, width), width)
@@ -327,7 +541,25 @@
         give(0, dqh, dq, t)
         if t >= 1:
             give_key(t - 1)
+        if t == 1:
+            add_x()
+        if t == n - 2:
+            add_z()
     give_key(n - 1)
+    load_w.wait()
+
+    def mix(i, carry):
+        cols = block(i, 2 * HEAD)
+        mixed[:, cols] = jnp.dot(
+            attn[...], wv[:, cols], preferred_element_type=jnp.float32
+        ).astype(jnp.bfloat16)
+        return carry
+
+    steps = mixed.shape[1] // (2 * HEAD)
+    lax.fori_loop(0, steps // 2, mix, 0)
+    add_last()
+    lax.fori_loop(steps // 2, steps, mix, 0)
+    take_shares()
     mine = pl.ds(pl.multiple_of(me * rows, rows), rows)
     for a, (src, dst) in enumerate(((dqh, dq), (dkh, dk), (dvh, dv))):
         for off in range(1, n):
@@ -357,34 +589,44 @@
     width = model_cols // n
     heads = width // HEAD
     bf16, f32 = jnp.bfloat16, jnp.float32
-    weight = lax.all_gather(out_weight, "dp", axis=0, tiled=True)
+    nz = lax.axis_size("dp") // 2
+    depth, out_cols = out_weight.shape
+    half = out_cols // 2
+    split = half // 2
+    piece = model_cols // (nz * n)
     hbm = pl.BlockSpec(memory_space=pl.ANY)
     vmem = pl.BlockSpec(memory_space=pltpu.VMEM)
     smem = pl.BlockSpec(memory_space=pltpu.SMEM)
     wide = jax.ShapeDtypeStruct((rows, model_cols), bf16)
     tall = jax.ShapeDtypeStruct((n * rows, width), bf16)
     level = jax.ShapeDtypeStruct((heads, n * rows, 1), f32)
-    attn, qh, kh, vh, ah, log_total = pl.pallas_call(
-        functools.partial(forward_kernel, n),
-        out_shape=(wide, tall, tall, tall, tall, level),
-        in_specs=[smem, hbm, hbm, hbm],
-        out_specs=(hbm, vmem, vmem, vmem, vmem, vmem),
+    half_grad = jax.ShapeDtypeStruct((rows, half), bf16)
+    full = jax.ShapeDtypeStruct((model_cols, out_cols), bf16)
+    attn, attn_other, g_other, weight, qh, kh, vh, ah, log_total = pl.pallas_call(
+        functools.partial(forward_kernel, n, nz),
+        out_shape=(wide, wide, half_grad, full, tall, tall, tall, tall, level),
+        in_specs=[smem] + [hbm] * 5,
+        out_specs=(hbm, hbm, hbm, hbm, vmem, vmem, vmem, vmem, vmem),
         scratch_shapes=[
-            sems(3, n), sems(3, n), sems(3), sems(n), sems(n), pltpu.SemaphoreType.DMA,
+            sems(3, n), sems(3, n), sems(4), sems(n), sems(n), pltpu.SemaphoreType.DMA,
+            sems(3), sems(3), sems(nz), sems(nz), sems(nz), sems(nz), sems(nz, n), sems(nz, n),
+            sems(nz, n), sems(nz, n), sems(nz), sems(nz),
         ],
         compiler_params=pltpu.CompilerParams(
             collective_id=0, has_side_effects=True, vmem_limit_bytes=50 * 2**20
         ),
         name="attend",
-    )(neighbours, query[0], key_in[0], value_in[0])
-    partial_weight = dot_tn(attn, upstream).astype(bf16)
-    piece = lax.psum_scatter(partial_weight, ("dp", "space"), scatter_dimension=0, tiled=True)
+    )(neighbours, query[0], key_in[0], value_in[0], upstream, out_weight)
     grad_attn = dot_nt(upstream, weight).astype(bf16)
-    dq, dk, dv = pl.pallas_call(
-        functools.partial(backward_kernel, n),
-        out_shape=(wide, wide, wide),
-        in_specs=[smem, hbm, vmem, vmem, vmem, vmem, vmem],
-        out_specs=(hbm, hbm, hbm),
+    dq, dk, dv, grad_weight, mixed = pl.pallas_call(
+        functools.partial(backward_kernel, n, nz),
+        out_shape=(
+            wide, wide, wide,
+            jax.ShapeDtypeStruct((depth, out_cols), bf16),
+            jax.ShapeDtypeStruct((rows, out_cols), bf16),
+        ),
+        in_specs=[smem, hbm] + [vmem] * 7 + [hbm, vmem, hbm],
+        out_specs=(hbm, hbm, hbm, hbm, vmem),
         scratch_shapes=[
             pltpu.VMEM(tall.shape, bf16),
             pltpu.VMEM(tall.shape, bf16),
@@ -392,15 +634,30 @@
             pltpu.VMEM(tall.shape, bf16),
             pltpu.VMEM(tall.shape, f32),
             pltpu.VMEM(tall.shape, f32),
+            pltpu.VMEM(full.shape, bf16),
+            pltpu.VMEM((rows, half), bf16),
+            pltpu.VMEM((nz, n, piece, split), bf16),
+            pltpu.VMEM((nz, n, piece, split), bf16),
+            pltpu.VMEM((n, nz, piece, split), bf16),
+            pltpu.VMEM((nz, piece, split), bf16),
+            pltpu.VMEM((nz, piece, split), bf16),
+            pltpu.VMEM((nz, n, piece, split), bf16),
+            pltpu.VMEM((n, piece, split), bf16),
+            pltpu.VMEM((n, piece, split), bf16),
+            pltpu.VMEM((piece, half), bf16),
             sems(1, n), sems(1, n), sems(1), sems(3, n), sems(3, n), sems(3),
+            sems(2), sems(n), sems(n), sems(nz), sems(nz), sems(nz), sems(nz), sems(n), sems(n),
+            sems(n), sems(2 * n), pltpu.SemaphoreType.DMA,
         ],
         compiler_params=pltpu.CompilerParams(
-            collective_id=1, has_side_effects=True, vmem_limit_bytes=50 * 2**20
+            collective_id=1, has_side_effects=True, vmem_limit_bytes=58 * 2**20
         ),
         name="attend_back",
-    )(neighbours, grad_attn, qh, kh, vh, ah, log_total)
-    mixed = jnp.dot(attn, weight, preferred_element_type=f32).astype(bf16)
-    grad_weight = lax.all_gather(piece, "space", axis=0, tiled=True).astype(f32)
+    )(
+        neighbours, grad_attn, qh, kh, vh, ah, log_total, attn, attn_other, upstream, g_other,
+        weight,
+    )
+    grad_weight = grad_weight.astype(f32)
     return (mixed[None], dq[None], dk[None], dv[None], grad_weight)
 
 
@@ -408,7 +665,7 @@
     n = mesh.shape["space"]
 
     def on_device(query, *rest):
-        if query.shape[2] % (n * HEAD) == 0:
+        if query.shape[2] % (n * HEAD) == 0 and n % 2 == 0 and mesh.shape["dp"] % 2 == 0:
             return heads_on_device(n, query, *rest)
         return halo_on_device(query, *rest)
 

time: 448 us -> 239 us (0.53)
  waiting for transfers between devices: 253 us -> 0 us
  Pallas kernels: 146 us -> 217 us
  matrix products: 24 us -> 7.53 us
  between operations: 13.8 us -> 0.68 us
    reduce_scatter x1 -> x0, waiting for transfers between devices: 136 us -> none  [heads_on_device(): lax.psum_scatter(partial_weight, ('dp', 'space'), scatter_dimension=0, ti...]
    all_gather x2 -> x0, waiting for transfers between devices: 115 us -> none  [the longest x1 88 us: heads_on_device(): weight = lax.all_gather(out_weight, 'dp', axis=0, tiled=True)]
    pallas_call x2, Pallas kernels: 146 us -> 217 us  [the longest x1 130 us: heads_on_device(): pl.pallas_call(functools.partial(backward_kernel, n, nz), out_shape=(wide...]
    dot_general x2 -> x0, matrix products: 16.5 us -> none  [the longest x1 8.73 us: heads_on_device(): mixed = jnp.dot(attn, weight, preferred_element_type=f32).astype(bf16)]
    unnamed x13 -> x22, local copies, waits for them, and re-layouts: 5.9 us -> 10.2 us
  transfers between devices with their start and end apart: 3 -> 0, of which waited for: 3 -> 0; matrix products, arithmetic and copies ran while one was open for 1% -> 0% of each run, Pallas kernels for 0% -> 0%
where the time goes in v2:
time: 239 us
  Pallas kernels  217 us (91%)
  local copies, waits for them, and re-layouts  10.2 us (4%)
  matrix products  7.53 us (3%)
  other arithmetic  3.09 us (1%)
    pallas_call x1, Pallas kernels, heads_on_device(): pl.pallas_call(functools.partial(backward_kernel, n, nz), out_shape=(wide...  130 us
    pallas_call x1, Pallas kernels, heads_on_device(): pl.pallas_call(functools.partial(forward_kernel, n, nz), out_shape=(wide,...  86.9 us
    unnamed x22, local copies, waits for them, and re-layouts  10.2 us
    dot_general x1, matrix products, dot_nt(): lax.dot_general(a, b, (((1,), (1,)), ((), ())), preferred_element_type=jn...  7.53 us

profile of v2, /device:TPU:14, one launch (start us, length us, event | category | flops | bytes accessed | tf_op | source)
XLA Modules:
  0.0 238.9 jit_solution(6073859133902910320)
XLA Ops:
  0.6 0.0 copy-start.3
  0.6 0.7 copy-done.3
  1.3 0.0 copy-start.4
  1.3 86.9 %attend.1 = (bf16[384,1536]{1,0:T(8,128)(2,1)S(1)}, bf16[384,1536]{1,0:T(8,128)(2,1)S(1)}, bf16[384,1536]{1,0:T(8,128)(2,1)S(1)}, bf16[1536,3072]{1,0:T(8,128)(2...) custom-call(s32[4,3]{1,0:T(4,128)S(1)} %copy-done.3, ...), custom_call_target="tpu_custom_call" | custom-call | tf_op jit(solution)/shard_map/attend/pallas_call | solution.py:605
  88.2 0.0 copy-start
  88.2 1.0 copy-done
  89.2 0.0 copy-start.1
  89.3 1.0 copy-done.1
  90.3 0.0 copy-start.2
  90.3 1.0 copy-done.2
  91.3 0.0 copy-done.4
  91.3 7.5 %fusion.ga = bf16[384,1536]{1,0:T(8,128)(2,1)} fusion(bf16[1536,3072]{1,0:T(8,128)(2,1)} %get-tuple-element.19.wf, bf16[1,384,3072]{2,1,0:T(8,128)(2,1)S(1)} %copy-done.4), kind=kOutput, calls=%fused_computation.1 | convolution fusion | flops 3624468480 | bytes 12976128 | tf_op jit(solution)/shard_map/dot_general | solution.py:155
  98.8 130.4 %attend_back.1 = (bf16[384,1536]{1,0:T(8,128)(2,1)}, bf16[384,1536]{1,0:T(8,128)(2,1)}, bf16[384,1536]{1,0:T(8,128)(2,1)}, bf16[192,3072]{1,0:T(8,128)(2,1)}, bf16[384,3072]{1,0:T(8,128)(2,1)}) custom-call(s32[4,3]{1,0:T(4,128)} %near.3, bf16[384,1536]{1,0:T(8,128)(2,1)} %fusion.ga, bf16[1536,384]{1,0:T(8,128)(2,1)} %get-tuple-element.20.qh, ...), custom_call_target="tpu_custom_call" | custom-call | tf_op jit(solution)/shard_map/attend_back/pallas_call | solution.py:621
  229.3 0.0 copy-start.5
  229.3 3.1 %convert_element_type.10 = f32[192,3072]{1,0:T(8,128)} convert(bf16[192,3072]{1,0:T(8,128)(2,1)} %get-tuple-element.32) | non-fusion elementwise | flops 589824 | bytes 3538944 | tf_op jit(solution)/shard_map/convert_element_type | solution.py:660
  232.4 0.0 copy-done.5
  232.4 0.0 copy-start.8
  232.4 1.4 copy.17
  233.8 0.7 copy-done.8
  234.5 0.0 copy-start.7
  234.5 1.0 copy.18
  235.5 0.7 copy-done.7
  236.2 0.0 copy-start.6
  236.2 1.0 copy.19
  237.2 0.7 copy-done.6
  237.8 1.0 copy.20
Async XLA Ops:
  0.6 0.7 copy-start.3
  1.3 90.0 %copy-start.4 = (bf16[1,384,3072]{2,1,0:T(8,128)(2,1)S(1)}, bf16[1,384,3072]{2,1,0:T(8,128)(2,1)}, u32[]{:S(2)}) copy-start(bf16[1,384,3072]{2,1,0:T(8,128)(2,1)} %param.10) | copy-start | bytes 7077892
  88.2 1.0 copy-start
  89.2 1.0 copy-start.1
  90.3 1.0 copy-start.2
  229.3 3.1 %copy-start.5 = (bf16[384,3072]{1,0:T(8,128)(2,1)S(1)}, bf16[384,3072]{1,0:T(8,128)(2,1)}, u32[]{:S(2)}) copy-start(bf16[384,3072]{1,0:T(8,128)(2,1)} %get-tuple-element.28) | copy-start | bytes 7077892
  232.4 2.1 copy-start.8
  234.5 1.7 copy-start.7
  236.2 1.7 copy-start.6

commit v3 on v0

--- a/solution.py
+++ b/solution.py
@@ -1,8 +1,11 @@
+import functools
 import math
 
 import jax
 import jax.numpy as jnp
 from jax import lax
+from jax.experimental import pallas as pl
+from jax.experimental.pallas import tpu as pltpu
 from jax.sharding import PartitionSpec as P
 
 HEAD = 128
@@ -24,7 +27,7 @@
     return x
 
 
-def on_device(query, key_in, value_in, out_weight, grad_out, neighbours):
+def halo_on_device(query, key_in, value_in, out_weight, grad_out, neighbours):
     query_rows = query[0]
     key_rows = key_in[0]
     value_rows = value_in[0]
@@ -133,7 +136,492 @@
     return (mixed[None], grad_query[None], grad_key[None], grad_value[None], grad_weight)
 
 
+MESH = pl.DeviceIdType.MESH
+SCALE = 1.0 / math.sqrt(HEAD)
+
+
+def window(tile, tiles):
+    return range(max(0, tile - 1), min(tiles, tile + 2))
+
+
+def tile_bias(near, tile, other):
+    live = near[tile, 0] == other
+    for slot in range(1, near.shape[1]):
+        live = jnp.logical_or(live, near[tile, slot] == other)
+    return jnp.where(live, 0.0, masked_score).astype(jnp.float32)
+
+
+def dot_nt(a, b):
+    return lax.dot_general(a, b, (((1,), (1,)), ((), ())), preferred_element_type=jnp.float32)
+
+
+def dot_tn(a, b):
+    return lax.dot_general(a, b, (((0,), (0,)), ((), ())), preferred_element_type=jnp.float32)
+
+
+def place(nz):
+    row = lax.axis_index("dp")
+    return row // 2, row % 2, lax.axis_index("space")
+
+
+def greet(peers):
+    barrier = pltpu.get_barrier_semaphore()
+    for row, column in peers:
+        pl.semaphore_signal(
+            barrier, inc=1, device_id={"dp": row, "space": column}, device_id_type=MESH
+        )
+    pl.semaphore_wait(barrier, len(peers))
+
+
+def send_to(src, dst, send_sem, recv_sem, row, column):
+    return pltpu.make_async_remote_copy(
+        src_ref=src,
+        dst_ref=dst,
+        send_sem=send_sem,
+        recv_sem=recv_sem,
+        device_id={"dp": row, "space": column},
+        device_id_type=MESH,
+    )
+
+
+def send(src, dst, send_sem, recv_sem, peer):
+    return send_to(src, dst, send_sem, recv_sem, lax.axis_index("dp"), peer)
+
+
+def block(index, size):
+    return pl.ds(pl.multiple_of(index * size, size), size)
+
+
+def layer_kernel(
+    n, nz, near, q, k, v, g, w, dq, dk, dv, gw, mixed,
+    attn, attn_other, gv, g_other, wf, ga, qh, kh, vh, ah, gh, dqh, dkh, dvh,
+    log_total, dk_sum, dv_sum, px, pz, xin, x_sum, xzin, zin, z_sum, zxin, total,
+    send_sem, recv_sem, own_sem, back_send, back_recv, back_own, load_sem,
+    core_send, core_recv, zq_send, zq_recv, zh_send, zh_recv, sq_send, sq_recv,
+    cq_send, cq_recv, ch_send, ch_recv,
+    xs, xr, xzs, xzr, zs, zr, zxs, zxr, fs, fr, f_own,
+):
+    z, core, me = place(nz)
+    mine_dp = 2 * z + core
+    twin = 2 * z + 1 - core
+    rows = q.shape[0]
+    width = qh.shape[1]
+    heads = width // HEAD
+    depth, model = w.shape
+    half = model // 2
+    quarter = half // n
+    split = px.shape[3]
+    rest = pz.shape[3]
+    piece = px.shape[2]
+    per = n // 2
+    heir = 2 * z + me // per
+    upper = pl.ds(half, half)
+    shard = block(mine_dp, depth)
+    my_quarter = block(me, quarter)
+    mine = block(me, rows)
+    bf16 = jnp.bfloat16
+
+    def column(o):
+        return lax.rem(me + o, n)
+
+    def line(o):
+        return 2 * lax.rem(z + o, nz) + core
+
+    def wide(ref):
+        return ref.astype(jnp.float32)
+
+    greet(
+        [(mine_dp, column(o)) for o in range(1, n)]
+        + [(line(o), me) for o in range(1, nz)]
+        + [(twin, column(o)) for o in range(n)]
+    )
+    done = []
+
+    def begin(copy):
+        copy.start()
+        done.append(copy)
+
+    def out_copy(a, src, dst, o, h):
+        peer = column(o)
+        return send(
+            src.at[:, block(peer * heads + h, HEAD)], dst.at[mine, block(h, HEAD)],
+            send_sem.at[a, o, h], recv_sem.at[a, o, h], peer,
+        )
+
+    def out_own(a, src, dst, h):
+        return pltpu.make_async_copy(
+            src.at[:, block(me * heads + h, HEAD)], dst.at[mine, block(h, HEAD)], own_sem.at[a, h]
+        )
+
+    def back_copy(a, src, dst, o, h):
+        peer = column(o)
+        return send(
+            src.at[block(peer, rows), block(h, HEAD)], dst.at[:, block(me * heads + h, HEAD)],
+            back_send.at[a, o, h], back_recv.at[a, o, h], peer,
+        )
+
+    def back_local(a, src, dst, h):
+        return pltpu.make_async_copy(
+            src.at[mine, block(h, HEAD)], dst.at[:, block(me * heads + h, HEAD)], back_own.at[a, h]
+        )
+
+    def give(a, src, dst, h):
+        for o in range(1, n):
+            back_copy(a, src, dst, o, h).start()
+        back_local(a, src, dst, h).start()
+
+    def take(a, src, dst, h):
+        for o in range(1, n):
+            back_copy(a, src, dst, o, h).wait()
+        back_local(a, src, dst, h).wait()
+
+    inputs = ((q, qh), (k, kh), (v, vh))
+
+    def start_head(h, carry):
+        for a, (src, dst) in enumerate(inputs):
+            for o in range(1, n):
+                out_copy(a, src, dst, o, h).start()
+            out_own(a, src, dst, h).start()
+        return carry
+
+    lax.fori_loop(0, 1, start_head, 0)
+    from_z, halves, quarters = [], [], []
+    for o in range(1, nz):
+        copy = send_to(
+            w.at[:, my_quarter], wf.at[shard, my_quarter], zq_send.at[o], zq_recv.at[o],
+            line(o), me,
+        )
+        copy.start()
+        from_z.append(copy)
+    lax.fori_loop(1, heads, start_head, 0)
+    for o in range(1, nz):
+        copy = send_to(
+            w.at[:, upper], wf.at[shard, upper], zh_send.at[o], zh_recv.at[o], line(o), me
+        )
+        copy.start()
+        halves.append(copy)
+    load_g = pltpu.make_async_copy(g, gv, load_sem.at[0])
+    load_g.start()
+    begin(pltpu.make_async_copy(w, wf.at[shard], load_sem.at[1]))
+    begin(send_to(w, wf.at[shard], core_send.at[0], core_recv.at[0], twin, me))
+    other_g = send_to(
+        g.at[:, block(1 - core, half)], g_other, core_send.at[1], core_recv.at[1], twin, me
+    )
+    other_g.start()
+
+    def theirs(o):
+        return block(line(nz - o), depth)
+
+    def pass_from_z():
+        for o in range(1, nz):
+            from_z[o - 1].wait()
+            part = wf.at[theirs(o), my_quarter]
+            for p in range(1, n):
+                send(part, part, sq_send.at[o, p], sq_recv.at[o, p], column(p)).start()
+            send_to(part, part, cq_send.at[o, 0], cq_recv.at[o, 0], twin, me).start()
+
+    def pass_quarters():
+        for o in range(1, nz):
+            part = wf.at[theirs(o), my_quarter]
+            for p in range(1, n):
+                send(part, part, sq_send.at[o, p], sq_recv.at[o, p], column(p)).wait()
+                came = wf.at[theirs(o), block(column(n - p), quarter)]
+                begin(send_to(came, came, cq_send.at[o, p], cq_recv.at[o, p], twin, me))
+            done.append(send_to(part, part, cq_send.at[o, 0], cq_recv.at[o, 0], twin, me))
+
+    def pass_halves():
+        for o in range(1, nz):
+            halves[o - 1].wait()
+            part = wf.at[theirs(o), upper]
+            begin(send_to(part, part, ch_send.at[o], ch_recv.at[o], twin, me))
+
+    def forward_head(h, carry):
+        for a, (src, dst) in enumerate(inputs):
+            for o in range(1, n):
+                out_copy(a, src, dst, o, h).wait()
+            out_own(a, src, dst, h).wait()
+        cols = block(h, HEAD)
+        for t in range(n):
+            here = pl.ds(t * rows, rows)
+            query = qh[here, cols]
+            scores = [
+                dot_nt(query, kh[pl.ds(u * rows, rows), cols]) * SCALE + tile_bias(near, t, u)
+                for u in window(t, n)
+            ]
+            top = functools.reduce(
+                jnp.maximum, [jnp.max(s, axis=1, keepdims=True) for s in scores]
+            )
+            parts = [jnp.exp(s - top) for s in scores]
+            summed = sum(jnp.sum(p, axis=1, keepdims=True) for p in parts)
+            out = sum(
+                jnp.dot(
+                    p.astype(bf16),
+                    vh[pl.ds(u * rows, rows), cols],
+                    preferred_element_type=jnp.float32,
+                )
+                for u, p in zip(window(t, n), parts)
+            )
+            ah[here, cols] = (out / summed).astype(bf16)
+            log_total[h, here, :] = top + jnp.log(summed)
+        give(0, ah, attn, h)
+        pl.when(h == 0)(pass_from_z)
+        return carry
+
+    lax.fori_loop(0, heads, forward_head, 0)
+    for h in range(heads):
+        take(0, ah, attn, h)
+    other_attn = send_to(attn, attn_other, core_send.at[2], core_recv.at[2], twin, me)
+    other_attn.start()
+    load_g.wait()
+    other_g.wait()
+    other_attn.wait()
+
+    def z_copy(o):
+        return send_to(
+            pz.at[lax.rem(z + o, nz)], zin.at[o], zs.at[o], zr.at[o], line(o), me
+        )
+
+    x_copies = [
+        send(px.at[:, column(o)], xin.at[o], xs.at[o], xr.at[o], column(o)) for o in range(1, n)
+    ]
+
+    def product(i, start, size):
+        cols = block(i, n * piece)
+        ours = gv[:, pl.ds(pl.multiple_of(core * half + start, HEAD), size)]
+        return dot_tn(attn[:, cols], ours) + dot_tn(
+            attn_other[:, cols], g_other[:, pl.ds(start, size)]
+        )
+
+    def z_part(i, carry):
+        o = i + 1
+        to = lax.rem(z + o, nz)
+        pz[to] = product(to, split, rest).astype(bf16).reshape(pz.shape[1:])
+
+        @pl.when(o < nz)
+        def _():
+            z_copy(o).start()
+
+        return carry
+
+    def x_part(i, carry):
+        px[i] = product(i, 0, split).astype(bf16).reshape(px.shape[1:])
+        return carry
+
+    lax.fori_loop(0, nz, z_part, 0)
+    pass_quarters()
+    lax.fori_loop(0, nz, x_part, 0)
+    for copy in x_copies:
+        copy.start()
+    pass_halves()
+    for copy in done:
+        copy.wait()
+
+    def project_back(i, carry):
+        o = i + 1
+        to = lax.rem(me + o, n)
+        cols = block(to, width)
+        ga[:, cols] = dot_nt(gv[...], wf[cols, :]).astype(bf16)
+
+        @pl.when(o < n)
+        def _():
+            for h in range(heads):
+                out_copy(3, ga, gh, o, h).start()
+
+        @pl.when(o == n)
+        def _():
+            for h in range(heads):
+                out_own(3, ga, gh, h).start()
+
+        return carry
+
+    lax.fori_loop(0, n, project_back, 0)
+
+    def mix(i, carry):
+        cols = block(i, 2 * HEAD)
+        mixed[:, cols] = jnp.dot(
+            attn[...], wf[:, cols], preferred_element_type=jnp.float32
+        ).astype(bf16)
+        return carry
+
+    steps = model // (2 * HEAD)
+    lax.fori_loop(0, steps // 2, mix, 0)
+
+    def xz_copy(o):
+        return send_to(
+            x_sum.at[lax.rem(z + o, nz)], xzin.at[o], xzs.at[o], xzr.at[o], line(o), me
+        )
+
+    def add_x():
+        for copy in x_copies:
+            copy.wait()
+        for i in range(nz):
+            x_sum[i] = (
+                wide(px[i, me]) + sum(wide(xin[o, i]) for o in range(1, n))
+            ).astype(bf16)
+        for o in range(1, nz):
+            xz_copy(o).start()
+
+    def backward_head(h, carry):
+        for o in range(1, n):
+            out_copy(3, ga, gh, o, h).wait()
+        out_own(3, ga, gh, h).wait()
+        cols = block(h, HEAD)
+        dk_sum[...] = jnp.zeros_like(dk_sum)
+        dv_sum[...] = jnp.zeros_like(dv_sum)
+        for t in range(n):
+            here = pl.ds(t * rows, rows)
+            query, grad = qh[here, cols], gh[here, cols]
+            level = log_total[h, here, :]
+            delta = jnp.sum(wide(grad) * wide(ah[here, cols]), axis=1, keepdims=True)
+            out = jnp.zeros((rows, HEAD), jnp.float32)
+            for u in window(t, n):
+                there = pl.ds(u * rows, rows)
+                key, value = kh[there, cols], vh[there, cols]
+                weight = jnp.exp(dot_nt(query, key) * SCALE + tile_bias(near, t, u) - level)
+                dscore = (weight * (dot_nt(grad, value) - delta) * SCALE).astype(bf16)
+                out += jnp.dot(dscore, key, preferred_element_type=jnp.float32)
+                dk_sum[there, :] += dot_tn(dscore, query)
+                dv_sum[there, :] += dot_tn(weight.astype(bf16), grad)
+            dqh[here, cols] = out.astype(bf16)
+        give(1, dqh, dq, h)
+        dkh[:, cols] = dk_sum[...].astype(bf16)
+        give(2, dkh, dk, h)
+        dvh[:, cols] = dv_sum[...].astype(bf16)
+        give(3, dvh, dv, h)
+        pl.when(h == 0)(add_x)
+        return carry
+
+    lax.fori_loop(0, heads, backward_head, 0)
+    for o in range(1, nz):
+        z_copy(o).wait()
+    for i in range(n):
+        z_sum[i] = (wide(pz[z, i]) + sum(wide(zin[o, i]) for o in range(1, nz))).astype(bf16)
+    zx_copies = [
+        send(z_sum.at[column(o)], zxin.at[o], zxs.at[o], zxr.at[o], column(o))
+        for o in range(1, n)
+    ]
+    for copy in zx_copies:
+        copy.start()
+    lax.fori_loop(steps // 2, steps, mix, 0)
+    for o in range(1, nz):
+        xz_copy(o).wait()
+    for copy in zx_copies:
+        copy.wait()
+    total[:, pl.ds(0, split)] = (
+        wide(x_sum[z]) + sum(wide(xzin[o]) for o in range(1, nz))
+    ).astype(bf16)
+    total[:, pl.ds(split, rest)] = (
+        wide(z_sum[me]) + sum(wide(zxin[o]) for o in range(1, n))
+    ).astype(bf16)
+    my_part = gw.at[block(lax.rem(me, per), piece), block(core, half)]
+
+    def shares(start):
+        for o in range(n):
+
+            def remote():
+                copy = send_to(total, my_part, fs.at[o], fr.at[core * n + me], heir, column(o))
+                copy.start() if start else copy.wait_send()
+
+            def local():
+                copy = pltpu.make_async_copy(total, my_part, f_own)
+                copy.start() if start else copy.wait()
+
+            if o > 0:
+                remote()
+            else:
+                pl.when(heir != mine_dp)(remote)
+                pl.when(heir == mine_dp)(local)
+
+    shares(True)
+    for h in range(heads):
+        take(1, dqh, dq, h)
+        take(2, dkh, dk, h)
+        take(3, dvh, dv, h)
+    shares(False)
+    for c in range(2):
+        for j in range(per):
+            source = core * per + j
+            part = gw.at[pl.ds(j * piece, piece), pl.ds(c * half, half)]
+
+            @pl.when(jnp.logical_or(source != me, core != c))
+            def _():
+                send_to(total, part, fs.at[0], fr.at[c * n + source], twin, me).wait_recv()
+
+
+def sems(*shape):
+    return pltpu.SemaphoreType.DMA(shape)
+
+
+def heads_on_device(n, query, key_in, value_in, out_weight, grad_out, neighbours):
+    upstream = grad_out[0]
+    rows, model_cols = query.shape[1:]
+    width = model_cols // n
+    heads = width // HEAD
+    bf16, f32 = jnp.bfloat16, jnp.float32
+    nz = lax.axis_size("dp") // 2
+    depth, out_cols = out_weight.shape
+    half = out_cols // 2
+    split = half // (3 * HEAD) * HEAD
+    piece = model_cols // (nz * n)
+    hbm = pl.BlockSpec(memory_space=pl.ANY)
+    vmem = pl.BlockSpec(memory_space=pltpu.VMEM)
+    smem = pl.BlockSpec(memory_space=pltpu.SMEM)
+    wide = jax.ShapeDtypeStruct((rows, model_cols), bf16)
+    tall = pltpu.VMEM((n * rows, width), bf16)
+    sums = pltpu.VMEM((n * rows, HEAD), f32)
+    rest = half - split
+    dq, dk, dv, grad_weight, mixed = pl.pallas_call(
+        functools.partial(layer_kernel, n, nz),
+        out_shape=(
+            wide, wide, wide,
+            jax.ShapeDtypeStruct((depth, out_cols), bf16),
+            jax.ShapeDtypeStruct((rows, out_cols), bf16),
+        ),
+        in_specs=[smem] + [hbm] * 5,
+        out_specs=(hbm, hbm, hbm, hbm, vmem),
+        scratch_shapes=[
+            pltpu.VMEM((rows, model_cols), bf16),
+            pltpu.VMEM((rows, model_cols), bf16),
+            pltpu.VMEM((rows, out_cols), bf16),
+            pltpu.VMEM((rows, half), bf16),
+            pltpu.VMEM((model_cols, out_cols), bf16),
+            pltpu.VMEM((rows, model_cols), bf16),
+            tall, tall, tall, tall, tall, tall, tall, tall,
+            pltpu.VMEM((heads, n * rows, 1), f32),
+            sums, sums,
+            pltpu.VMEM((nz, n, piece, split), bf16),
+            pltpu.VMEM((nz, n, piece, rest), bf16),
+            pltpu.VMEM((n, nz, piece, split), bf16),
+            pltpu.VMEM((nz, piece, split), bf16),
+            pltpu.VMEM((nz, piece, split), bf16),
+            pltpu.VMEM((nz, n, piece, rest), bf16),
+            pltpu.VMEM((n, piece, rest), bf16),
+            pltpu.VMEM((n, piece, rest), bf16),
+            pltpu.VMEM((piece, half), bf16),
+            sems(4, n, heads), sems(4, n, heads), sems(4, heads),
+            sems(4, n, heads), sems(4, n, heads), sems(4, heads), sems(2),
+            sems(3), sems(3), sems(nz), sems(nz), sems(nz), sems(nz), sems(nz, n), sems(nz, n),
+            sems(nz, n), sems(nz, n), sems(nz), sems(nz),
+            sems(n), sems(n), sems(nz), sems(nz), sems(nz), sems(nz), sems(n), sems(n),
+            sems(n), sems(2 * n), pltpu.SemaphoreType.DMA,
+        ],
+        compiler_params=pltpu.CompilerParams(
+            collective_id=0, has_side_effects=True, vmem_limit_bytes=60 * 2**20
+        ),
+        name="layer",
+    )(neighbours, query[0], key_in[0], value_in[0], upstream, out_weight)
+    grad_weight = grad_weight.astype(f32)
+    return (mixed[None], dq[None], dk[None], dv[None], grad_weight)
+
+
 def solution(mesh):
+    n = mesh.shape["space"]
+
+    def on_device(query, *rest):
+        if query.shape[2] % (n * HEAD) == 0 and n % 2 == 0 and mesh.shape["dp"] % 2 == 0:
+            return heads_on_device(n, query, *rest)
+        return halo_on_device(query, *rest)
+
     return jax.shard_map(
         on_device,
         mesh=mesh,

time: 452 us -> 197 us (0.44)
  waiting for transfers between devices: 252 us -> 0 us
  Pallas kernels: 0 us -> 184 us
  matrix products: 104 us -> 0 us
  local copies, waits for them, and re-layouts: 38.3 us -> 6.51 us
  other arithmetic: 22.8 us -> 3.09 us
  starting transfers between devices: 17 us -> 0 us
  between operations: 13.9 us -> 0.66 us
    pallas_call x0 -> x1, Pallas kernels: none -> 184 us  [heads_on_device(): pl.pallas_call(functools.partial(layer_kernel, n, nz), out_shape=(wide, w...]
    ppermute x6 -> x0, waiting for transfers between devices: 181 us -> none  [the longest x3 124 us: padded(): before = lax.ppermute(last, axis, up)]
    dot_general x9 -> x0, matrix products: 104 us -> none  [the longest x1 16.7 us: on_device(): jnp.einsum('hij,jhd->ihd', dscore, key_heads, preferred_element_type=jnp....]
    reduce_scatter x1 -> x0, waiting for transfers between devices: 61.5 us -> none  [on_device(): lax.psum_scatter(lax.dot_general(attn_cols, upstream, (((0,), (0,)), ((),...]
    slice x4 -> x0, local copies, waits for them, and re-layouts: 17.3 us -> none  [the longest x2 9.21 us: on_device(): far_grads = query_near[1].reshape(3 * tile_rows, head_count, HEAD)]
    ppermute x6 -> x0, starting transfers between devices: 16.9 us -> none  [the longest x3 12.9 us: padded(): after = lax.ppermute(initial, axis, down)]
    unnamed x29 -> x12, local copies, waits for them, and re-layouts: 17.1 us -> 6.51 us
    reduce_sum x1 -> x0, other arithmetic: 8.79 us -> none  [on_device(): jnp.sum(jnp.exp(scores - row_max), axis=2, keepdims=True)]
  transfers between devices with their start and end apart: 9 -> 0, of which waited for: 6 -> 0; matrix products, arithmetic and copies ran while one was open for 29% -> 0% of each run, Pallas kernels for 0% -> 0%
where the time goes in v3:
time: 197 us; the launch traced here: 194 us
  Pallas kernels  184 us (93%)
  local copies, waits for them, and re-layouts  6.51 us (3%)
  other arithmetic  3.09 us (2%)
    pallas_call x1, Pallas kernels, heads_on_device(): pl.pallas_call(functools.partial(layer_kernel, n, nz), out_shape=(wide, w...  184 us
    unnamed x12, local copies, waits for them, and re-layouts  6.51 us

profile of v3, /device:TPU:14, one launch (start us, length us, event | category | flops | bytes accessed | tf_op | source)
XLA Modules:
  0.0 194.3 jit_solution(602823090072541140)
XLA Ops:
  0.6 184.1 %layer.1 = (bf16[384,1536]{1,0:T(8,128)(2,1)}, bf16[384,1536]{1,0:T(8,128)(2,1)}, bf16[384,1536]{1,0:T(8,128)(2,1)}, bf16[192,3072]{1,0:T(8,128)(2,1)}, bf16[384,3072]{1,0:T(8,128)(2,1)}) custom-call(s32[4,3]{1,0:T(4,128)} %near.1, bf16[384,1536]{1,0:T(8,128)(2,1)} %bitcast.13, bf16[384,1536]{1,0:T(8,128)(2,1)} %bitcast.14, bf16[384,1536]{1,0:T(8,128)(2,1)} %bitcast.15, ...), custom_call_target="tpu_custom_call" | custom-call | tf_op jit(solution)/shard_map/layer/pallas_call | solution.py:573
  184.7 0.0 copy-start
  184.7 3.1 %convert_element_type.3 = f32[192,3072]{1,0:T(8,128)} convert(bf16[192,3072]{1,0:T(8,128)(2,1)} %get-tuple-element.14) | non-fusion elementwise | flops 589824 | bytes 3538944 | tf_op jit(solution)/shard_map/convert_element_type | solution.py:613
  187.8 0.0 copy-done
  187.8 0.0 copy-start.3
  187.8 1.4 copy.15
  189.2 0.7 copy-done.3
  189.9 0.0 copy-start.2
  189.9 1.0 copy.16
  190.9 0.7 copy-done.2
  191.6 0.0 copy-start.1
  191.6 1.0 copy.17
  192.6 0.7 copy-done.1
  193.3 1.0 copy.18
Async XLA Ops:
  184.7 3.1 %copy-start = (bf16[384,3072]{1,0:T(8,128)(2,1)S(1)}, bf16[384,3072]{1,0:T(8,128)(2,1)}, u32[]{:S(2)}) copy-start(bf16[384,3072]{1,0:T(8,128)(2,1)} %get-tuple-element.10) | copy-start | bytes 7077892
  187.8 2.1 %copy-start.3 = (bf16[384,1536]{1,0:T(8,128)(2,1)S(1)}, bf16[384,1536]{1,0:T(8,128)(2,1)}, u32[]{:S(2)}) copy-start(bf16[384,1536]{1,0:T(8,128)(2,1)} %get-tuple-element.11) | copy-start | bytes 3538948
  189.9 1.7 copy-start.2
  191.6 1.7 copy-start.1

commit v4 on v3

--- a/solution.py
+++ b/solution.py
@@ -345,26 +345,22 @@
             here = pl.ds(t * rows, rows)
             query = qh[here, cols]
             scores = [
-                dot_nt(query, kh[pl.ds(u * rows, rows), cols]) * SCALE + tile_bias(near, t, u)
+                dot_nt(kh[pl.ds(u * rows, rows), cols], query) * SCALE + tile_bias(near, t, u)
                 for u in window(t, n)
             ]
             top = functools.reduce(
-                jnp.maximum, [jnp.max(s, axis=1, keepdims=True) for s in scores]
+                jnp.maximum, [jnp.max(s, axis=0, keepdims=True) for s in scores]
             )
             parts = [jnp.exp(s - top) for s in scores]
-            summed = sum(jnp.sum(p, axis=1, keepdims=True) for p in parts)
+            summed = sum(jnp.sum(p, axis=0, keepdims=True) for p in parts)
             out = sum(
-                jnp.dot(
-                    p.astype(bf16),
-                    vh[pl.ds(u * rows, rows), cols],
-                    preferred_element_type=jnp.float32,
-                )
+                dot_tn(vh[pl.ds(u * rows, rows), cols], p.astype(bf16))
                 for u, p in zip(window(t, n), parts)
             )
-            ah[here, cols] = (out / summed).astype(bf16)
-            log_total[h, here, :] = top + jnp.log(summed)
+            ah[here, cols] = jnp.transpose(out / summed).astype(bf16)
+            log_total[h, t] = top + jnp.log(summed)
         give(0, ah, attn, h)
-        pl.when(h == 0)(pass_from_z)
+        pl.when(h == heads - 1)(pass_from_z)
         return carry
 
     lax.fori_loop(0, heads, forward_head, 0)
@@ -408,10 +404,8 @@
         return carry
 
     lax.fori_loop(0, nz, z_part, 0)
+    lax.fori_loop(0, nz, x_part, 0)
     pass_quarters()
-    lax.fori_loop(0, nz, x_part, 0)
-    for copy in x_copies:
-        copy.start()
     pass_halves()
     for copy in done:
         copy.wait()
@@ -435,6 +429,8 @@
         return carry
 
     lax.fori_loop(0, n, project_back, 0)
+    for copy in x_copies:
+        copy.start()
 
     def mix(i, carry):
         cols = block(i, 2 * HEAD)
@@ -471,24 +467,28 @@
         for t in range(n):
             here = pl.ds(t * rows, rows)
             query, grad = qh[here, cols], gh[here, cols]
-            level = log_total[h, here, :]
-            delta = jnp.sum(wide(grad) * wide(ah[here, cols]), axis=1, keepdims=True)
-            out = jnp.zeros((rows, HEAD), jnp.float32)
+            level = log_total[h, t]
+            delta = jnp.sum(
+                jnp.transpose(wide(grad) * wide(ah[here, cols])), axis=0, keepdims=True
+            )
+            out = jnp.zeros((HEAD, rows), jnp.float32)
             for u in window(t, n):
                 there = pl.ds(u * rows, rows)
                 key, value = kh[there, cols], vh[there, cols]
-                weight = jnp.exp(dot_nt(query, key) * SCALE + tile_bias(near, t, u) - level)
-                dscore = (weight * (dot_nt(grad, value) - delta) * SCALE).astype(bf16)
-                out += jnp.dot(dscore, key, preferred_element_type=jnp.float32)
-                dk_sum[there, :] += dot_tn(dscore, query)
-                dv_sum[there, :] += dot_tn(weight.astype(bf16), grad)
-            dqh[here, cols] = out.astype(bf16)
+                weight = jnp.exp(dot_nt(key, query) * SCALE + (tile_bias(near, t, u) - level))
+                dscore = (weight * (dot_nt(value, grad) - delta) * SCALE).astype(bf16)
+                out += dot_tn(key, dscore)
+                dk_sum[there, :] += jnp.dot(dscore, query, preferred_element_type=jnp.float32)
+                dv_sum[there, :] += jnp.dot(
+                    weight.astype(bf16), grad, preferred_element_type=jnp.float32
+                )
+            dqh[here, cols] = jnp.transpose(out).astype(bf16)
         give(1, dqh, dq, h)
         dkh[:, cols] = dk_sum[...].astype(bf16)
         give(2, dkh, dk, h)
         dvh[:, cols] = dv_sum[...].astype(bf16)
         give(3, dvh, dv, h)
-        pl.when(h == 0)(add_x)
+        pl.when(h == min(1, heads - 1))(add_x)
         return carry
 
     lax.fori_loop(0, heads, backward_head, 0)
@@ -587,7 +587,7 @@
             pltpu.VMEM((model_cols, out_cols), bf16),
             pltpu.VMEM((rows, model_cols), bf16),
             tall, tall, tall, tall, tall, tall, tall, tall,
-            pltpu.VMEM((heads, n * rows, 1), f32),
+            pltpu.VMEM((heads, n, 1, rows), f32),
             sums, sums,
             pltpu.VMEM((nz, n, piece, split), bf16),
             pltpu.VMEM((nz, n, piece, rest), bf16),

time: 197 us -> 216 us (1.096)
  Pallas kernels: 184 us -> 204 us
    pallas_call x1, Pallas kernels: 184 us -> 204 us  [heads_on_device(): pl.pallas_call(functools.partial(layer_kernel, n, nz), out_shape=(wide, w...]
where the time goes in v4:
time: 216 us; the launch traced here: 214 us
  Pallas kernels  204 us (94%)
  local copies, waits for them, and re-layouts  6.51 us (3%)
  other arithmetic  3.09 us (1%)
    pallas_call x1, Pallas kernels, heads_on_device(): pl.pallas_call(functools.partial(layer_kernel, n, nz), out_shape=(wide, w...  204 us
    unnamed x12, local copies, waits for them, and re-layouts  6.51 us

profile of v4, /device:TPU:14, one launch (start us, length us, event | category | flops | bytes accessed | tf_op | source)
XLA Modules:
  0.0 214.2 jit_solution(6222679050029452607)
XLA Ops:
  0.6 203.9 %layer.1 = (bf16[384,1536]{1,0:T(8,128)(2,1)}, bf16[384,1536]{1,0:T(8,128)(2,1)}, bf16[384,1536]{1,0:T(8,128)(2,1)}, bf16[192,3072]{1,0:T(8,128)(2,1)}, bf16[384,3072]{1,0:T(8,128)(2,1)}) custom-call(s32[4,3]{1,0:T(4,128)} %near.1, bf16[384,1536]{1,0:T(8,128)(2,1)} %bitcast.13, bf16[384,1536]{1,0:T(8,128)(2,1)} %bitcast.14, bf16[384,1536]{1,0:T(8,128)(2,1)} %bitcast.15, ...), custom_call_target="tpu_custom_call" | custom-call | tf_op jit(solution)/shard_map/layer/pallas_call | solution.py:573
  204.6 0.0 copy-start
  204.6 3.1 %convert_element_type.3 = f32[192,3072]{1,0:T(8,128)} convert(bf16[192,3072]{1,0:T(8,128)(2,1)} %get-tuple-element.14) | non-fusion elementwise | flops 589824 | bytes 3538944 | tf_op jit(solution)/shard_map/convert_element_type | solution.py:613
  207.7 0.0 copy-done
  207.7 0.0 copy-start.3
  207.7 1.4 copy.15
  209.1 0.7 copy-done.3
  209.8 0.0 copy-start.2
  209.8 1.0 copy.16
  210.8 0.7 copy-done.2
  211.5 0.0 copy-start.1
  211.5 1.0 copy.17
  212.5 0.7 copy-done.1
  213.2 1.0 copy.18
Async XLA Ops:
  204.6 3.1 %copy-start = (bf16[384,3072]{1,0:T(8,128)(2,1)S(1)}, bf16[384,3072]{1,0:T(8,128)(2,1)}, u32[]{:S(2)}) copy-start(bf16[384,3072]{1,0:T(8,128)(2,1)} %get-tuple-element.10) | copy-start | bytes 7077892
  207.7 2.1 copy-start.3
  209.8 1.7 copy-start.2
  211.5 1.7 copy-start.1

commit v5 on v3

--- a/solution.py
+++ b/solution.py
@@ -362,7 +362,8 @@
                 for u, p in zip(window(t, n), parts)
             )
             ah[here, cols] = (out / summed).astype(bf16)
-            log_total[h, here, :] = top + jnp.log(summed)
+            level = jnp.broadcast_to(top + jnp.log(summed), (rows, HEAD))
+            log_total[h, t] = jnp.transpose(level)[0:1, :]
         give(0, ah, attn, h)
         pl.when(h == 0)(pass_from_z)
         return carry
@@ -471,17 +472,21 @@
         for t in range(n):
             here = pl.ds(t * rows, rows)
             query, grad = qh[here, cols], gh[here, cols]
-            level = log_total[h, here, :]
-            delta = jnp.sum(wide(grad) * wide(ah[here, cols]), axis=1, keepdims=True)
+            level = log_total[h, t]
+            delta = jnp.sum(
+                jnp.transpose(wide(grad) * wide(ah[here, cols])), axis=0, keepdims=True
+            )
             out = jnp.zeros((rows, HEAD), jnp.float32)
             for u in window(t, n):
                 there = pl.ds(u * rows, rows)
                 key, value = kh[there, cols], vh[there, cols]
-                weight = jnp.exp(dot_nt(query, key) * SCALE + tile_bias(near, t, u) - level)
-                dscore = (weight * (dot_nt(grad, value) - delta) * SCALE).astype(bf16)
-                out += jnp.dot(dscore, key, preferred_element_type=jnp.float32)
-                dk_sum[there, :] += dot_tn(dscore, query)
-                dv_sum[there, :] += dot_tn(weight.astype(bf16), grad)
+                weight = jnp.exp(dot_nt(key, query) * SCALE + (tile_bias(near, t, u) - level))
+                dscore = (weight * (dot_nt(value, grad) - delta) * SCALE).astype(bf16)
+                out += dot_tn(dscore, key)
+                dk_sum[there, :] += jnp.dot(dscore, query, preferred_element_type=jnp.float32)
+                dv_sum[there, :] += jnp.dot(
+                    weight.astype(bf16), grad, preferred_element_type=jnp.float32
+                )
             dqh[here, cols] = out.astype(bf16)
         give(1, dqh, dq, h)
         dkh[:, cols] = dk_sum[...].astype(bf16)
@@ -587,7 +592,7 @@
             pltpu.VMEM((model_cols, out_cols), bf16),
             pltpu.VMEM((rows, model_cols), bf16),
             tall, tall, tall, tall, tall, tall, tall, tall,
-            pltpu.VMEM((heads, n * rows, 1), f32),
+            pltpu.VMEM((heads, n, 1, rows), f32),
             sums, sums,
             pltpu.VMEM((nz, n, piece, split), bf16),
             pltpu.VMEM((nz, n, piece, rest), bf16),

time: 197 us -> 197 us (level)
  no operation moved by 1% of the time
where the time goes in v5:
time: 197 us; the launch traced here: 194 us
  Pallas kernels  184 us (93%)
  local copies, waits for them, and re-layouts  6.51 us (3%)
  other arithmetic  3.09 us (2%)
    pallas_call x1, Pallas kernels, heads_on_device(): pl.pallas_call(functools.partial(layer_kernel, n, nz), out_shape=(wide, w...  184 us
    unnamed x12, local copies, waits for them, and re-layouts  6.51 us

profile of v5, /device:TPU:14, one launch (start us, length us, event | category | flops | bytes accessed | tf_op | source)
XLA Modules:
  0.0 194.3 jit_solution(4517458814506721500)
XLA Ops:
  0.6 184.1 %layer.1 = (bf16[384,1536]{1,0:T(8,128)(2,1)}, bf16[384,1536]{1,0:T(8,128)(2,1)}, bf16[384,1536]{1,0:T(8,128)(2,1)}, bf16[192,3072]{1,0:T(8,128)(2,1)}, bf16[384,3072]{1,0:T(8,128)(2,1)}) custom-call(s32[4,3]{1,0:T(4,128)} %near.1, bf16[384,1536]{1,0:T(8,128)(2,1)} %bitcast.13, bf16[384,1536]{1,0:T(8,128)(2,1)} %bitcast.14, bf16[384,1536]{1,0:T(8,128)(2,1)} %bitcast.15, ...), custom_call_target="tpu_custom_call" | custom-call | tf_op jit(solution)/shard_map/layer/pallas_call | solution.py:578
  184.7 0.0 copy-start
  184.7 3.1 %convert_element_type.3 = f32[192,3072]{1,0:T(8,128)} convert(bf16[192,3072]{1,0:T(8,128)(2,1)} %get-tuple-element.14) | non-fusion elementwise | flops 589824 | bytes 3538944 | tf_op jit(solution)/shard_map/convert_element_type | solution.py:618
  187.8 0.0 copy-done
  187.8 0.0 copy-start.3
  187.8 1.4 copy.15
  189.2 0.7 copy-done.3
  189.9 0.0 copy-start.2
  189.9 1.0 copy.16
  190.9 0.7 copy-done.2
  191.6 0.0 copy-start.1
  191.6 1.0 copy.17
  192.6 0.7 copy-done.1
  193.3 1.0 copy.18
Async XLA Ops:
  184.7 3.1 %copy-start = (bf16[384,3072]{1,0:T(8,128)(2,1)S(1)}, bf16[384,3072]{1,0:T(8,128)(2,1)}, u32[]{:S(2)}) copy-start(bf16[384,3072]{1,0:T(8,128)(2,1)} %get-tuple-element.10) | copy-start | bytes 7077892
  187.8 2.1 %copy-start.3 = (bf16[384,1536]{1,0:T(8,128)(2,1)S(1)}, bf16[384,1536]{1,0:T(8,128)(2,1)}, u32[]{:S(2)}) copy-start(bf16[384,1536]{1,0:T(8,128)(2,1)} %get-tuple-element.11) | copy-start | bytes 3538948
  189.9 1.7 copy-start.2
  191.6 1.7 copy-start.1
